TPU v7x, 32 devices: a whole 2x2x4 slice. The times are simulated.
32 devices in a mesh: dp: 4 (over x, core), fsdp: 8 (over z, y).
Axes of the slice: x: 2, y: 2, z: 4, core: 2. Of those that a mesh axis runs over, the one named last changes fastest.
Arguments:
- tokens: bfloat16 [32, 1024, 768], P(('dp', 'fsdp')), may hold values from -6 to 6
- lengths: int32 [32, 8], P(('dp', 'fsdp')), may hold values from 1 to 256, 896 in all within a row
- lead_index: int32 [32, 8], P(('dp', 'fsdp')), may hold values from 0 to 19
- cotangent: bfloat16 [32, 1024, 768], P(('dp', 'fsdp')), may hold values from -6 to 6
- qkv_weight: bfloat16 [768, 2304], P('dp', 'fsdp'), may hold values from -0.21875 to 0.21875
- out_weight: bfloat16 [768, 768], P('dp', 'fsdp'), may hold values from -2 to 2
- up_weight: bfloat16 [768, 3072], P('dp', 'fsdp'), may hold values from -0.21875 to 0.21875
- down_weight: bfloat16 [3072, 768], P('dp', 'fsdp'), may hold values from -0.109375 to 0.109375
- vectors: bfloat16 [8, 768], P('dp', 'fsdp'), may hold values from -1.75 to 1.75
- lead_table: bfloat16 [20, 768], P('dp', 'fsdp'), may hold values from -3 to 3
- up_bias: bfloat16 [4, 768], P('dp', 'fsdp'), may hold values from -1.75 to 1.75
Outputs:
- block_output: bfloat16 [32, 1024, 768], P(('dp', 'fsdp'))
- input_grad: float32 [32, 1024, 768], P(('dp', 'fsdp'))
- qkv_grad: float32 [768, 2304], P('dp', 'fsdp')
- out_grad: float32 [768, 768], P('dp', 'fsdp')
- up_grad: float32 [768, 3072], P('dp', 'fsdp')
- down_grad: float32 [3072, 768], P('dp', 'fsdp')
- vectors_grad: float32 [8, 768], P('dp', 'fsdp')
- table_grad: float32 [20, 768], P('dp', 'fsdp')
- up_bias_grad: float32 [4, 768], P('dp', 'fsdp')
Inputs may be any that keep to these rules, and one draw needn't show every extreme that they name: `lengths`: the 8 windows of a row hold 896 patches together, the longest exactly 256; the last 128 positions of every row are padding.
All inputs are finite; a program needn't handle non-finite values.
Results may differ from a plain program's by a relative error of at most 0.012.
Values may be sent and summed in bfloat16 or wider, within the bound.
No kernel may reach another device: no remote copies, remote signals or barrier semaphores. Data moves between devices by JAX's collectives and lax.ppermute only.
A program may use at most 256 MiB of HBM per device.

v0:
```python
import jax
import jax.numpy as jnp
from jax import lax
from jax.sharding import PartitionSpec as P

D = 768
HEADS = 12
HD = 64
FF = 3072
LEADS = 20
WIN = 8
L = 1024


EPSILON = 1e-05
MASKED = -1e30


def layer_norm(values, gain_off, shift_by):
    center = values - jnp.mean(values, axis=-1, keepdims=True)
    spread = jnp.mean(center * center, axis=-1, keepdims=True)
    return center * lax.rsqrt(spread + EPSILON) * (1.0 + gain_off) + shift_by


def smooth_gate(values):
    return jax.nn.gelu(values, approximate=False)


def window_index(lengths):
    bounds = jnp.cumsum(lengths)
    places = jnp.arange(L, dtype=jnp.int32)
    return jnp.sum((places[:, None] >= bounds[None, :]).astype(jnp.int32), axis=1)


def lead_onehot(windows, lead_index):
    chosen = windows[:, None] == jnp.arange(WIN, dtype=jnp.int32)[None, :]
    lead_token = jnp.sum(jnp.where(chosen, lead_index[None, :], 0), axis=1)
    lead_token = jnp.where(windows < WIN, lead_token, -1)
    return (lead_token[:, None] == jnp.arange(LEADS, dtype=jnp.int32)[None, :]).astype(jnp.float32)


def contract_rows(left_side, right_side):
    return lax.dot_general(
        left_side, right_side, (((0,), (0,)), ((), ())), preferred_element_type=jnp.float32
    )


def contract_cols(left_side, right_side):
    return lax.dot_general(
        left_side, right_side, (((1,), (1,)), ((), ())), preferred_element_type=jnp.float32
    )


def collect(shards):
    across = (
        lax.all_gather(shards[0], "dp", axis=0, tiled=True),
        lax.all_gather(shards[1], "dp", axis=0, tiled=True),
        lax.all_gather(shards[2], "dp", axis=0, tiled=True),
        lax.all_gather(shards[3], "dp", axis=0, tiled=True),
        lax.all_gather(shards[4], "dp", axis=0, tiled=True),
        lax.all_gather(shards[5], "dp", axis=0, tiled=True),
        lax.all_gather(shards[6], "dp", axis=0, tiled=True),
    )
    return (
        lax.all_gather(across[0], "fsdp", axis=1, tiled=True),
        lax.all_gather(across[1], "fsdp", axis=1, tiled=True),
        lax.all_gather(across[2], "fsdp", axis=1, tiled=True),
        lax.all_gather(across[3], "fsdp", axis=1, tiled=True),
        lax.all_gather(across[4], "fsdp", axis=1, tiled=True),
        lax.all_gather(across[5], "fsdp", axis=1, tiled=True),
        lax.all_gather(across[6], "fsdp", axis=1, tiled=True),
    )


def masked_scores(query_block, key_heads, window_block, window_row):
    raw_scores = jnp.einsum(
        "qhd,khd->hqk", query_block, key_heads, preferred_element_type=jnp.float32
    ) * HD ** (-0.5)
    visible = window_block[:, None] == window_row[None, :]
    return jnp.where(visible[None], raw_scores, MASKED)


def attend_row(operands):
    packed_row, window_row = operands
    block_len = min(512, L)
    count = L // block_len
    query_blocks = packed_row[:, 0].reshape(count, block_len, HEADS, HD)
    window_blocks = window_row.reshape(count, block_len)
    key_heads = packed_row[:, 1]
    value_heads = packed_row[:, 2]

    def attend_block(paired):
        query_block, window_block = paired
        scores = masked_scores(query_block, key_heads, window_block, window_row)
        row_max = jnp.max(scores, axis=-1, keepdims=True)
        exponent = jnp.exp(scores - row_max)
        denominator = jnp.sum(exponent, axis=-1, keepdims=True)
        softmaxed = (exponent / denominator).astype(jnp.bfloat16)
        mixture = jnp.einsum(
            "hqk,khd->qhd", softmaxed, value_heads, preferred_element_type=jnp.float32
        )
        return (mixture, (row_max + jnp.log(denominator))[..., 0])

    mixture, log_total = lax.map(attend_block, (query_blocks, window_blocks))
    return (mixture.reshape(L, HEADS, HD), log_total)


def attend_back_row(operands):
    packed_row, window_row, grad_row, log_row = operands
    block_len = min(512, L)
    count = L // block_len
    query_blocks = packed_row[:, 0].reshape(count, block_len, HEADS, HD)
    key_heads = packed_row[:, 1]
    value_heads = packed_row[:, 2]
    grad_blocks = grad_row.reshape(count, block_len, HEADS, HD)
    window_blocks = window_row.reshape(count, block_len)
    scale = HD ** (-0.5)

    def back_block(running, pieces):
        query_block, grad_block, window_block, log_block = pieces
        scores = masked_scores(query_block, key_heads, window_block, window_row)
        soft_full = jnp.exp(scores - log_block[..., None])
        softmaxed = soft_full.astype(jnp.bfloat16)
        grad_soft = jnp.einsum(
            "qhd,khd->hqk", grad_block, value_heads, preferred_element_type=jnp.float32
        )
        grad_scores = soft_full * (
            grad_soft - jnp.sum(soft_full * grad_soft, axis=-1, keepdims=True)
        )
        grad_scores = grad_scores.astype(jnp.bfloat16)
        grad_query = (
            jnp.einsum("hqk,khd->qhd", grad_scores, key_heads, preferred_element_type=jnp.float32)
            * scale
        )
        grad_keys = (
            running[0]
            + jnp.einsum(
                "hqk,qhd->khd", grad_scores, query_block, preferred_element_type=jnp.float32
            )
            * scale
        )
        grad_values = running[1] + jnp.einsum(
            "hqk,qhd->khd", softmaxed, grad_block, preferred_element_type=jnp.float32
        )
        return ((grad_keys, grad_values), grad_query)

    zeros_start = jnp.zeros((L, HEADS, HD), jnp.float32)
    (grad_keys, grad_values), grad_query = lax.scan(
        back_block, (zeros_start, zeros_start), (query_blocks, grad_blocks, window_blocks, log_row)
    )
    return jnp.stack([grad_query.reshape(L, HEADS, HD), grad_keys, grad_values], axis=1)


def per_device(
    tokens,
    lengths,
    lead_index,
    cotangent,
    qkv_weight,
    out_weight,
    up_weight,
    down_weight,
    vectors,
    lead_table,
    up_bias,
):
    shard_list = (qkv_weight, out_weight, up_weight, down_weight, vectors, lead_table, up_bias)
    gathered = collect(shard_list)
    full_qkv, full_out, full_up, full_down, full_vec, full_table, full_upb = gathered
    vector_f32 = full_vec.astype(jnp.float32)
    up_shift = full_upb.astype(jnp.float32).reshape(FF)
    row_count = tokens.shape[0]
    total_tok = row_count * L
    windows = jax.vmap(window_index)(lengths)
    onehots = jax.vmap(lead_onehot)(windows, lead_index)
    flat_onehot = onehots.reshape(total_tok, LEADS)
    inputs = tokens.astype(jnp.float32).reshape(total_tok, D)
    embedded = jnp.dot(
        flat_onehot.astype(jnp.bfloat16), full_table, preferred_element_type=jnp.float32
    )
    normed_one = (layer_norm(inputs, vector_f32[0], vector_f32[1]) + embedded).astype(jnp.bfloat16)
    qkv_bias = jnp.concatenate([vector_f32[4], jnp.zeros((D,), jnp.float32), vector_f32[5]])
    packed = (jnp.dot(normed_one, full_qkv, preferred_element_type=jnp.float32) + qkv_bias).astype(
        jnp.bfloat16
    )
    heads_view = packed.reshape(row_count, L, 3, HEADS, HD)
    mixture, log_total = lax.map(attend_row, (heads_view, windows))
    mixed_flat = mixture.reshape(total_tok, D).astype(jnp.bfloat16)
    attended = jnp.dot(mixed_flat, full_out, preferred_element_type=jnp.float32) + vector_f32[6]
    middle = inputs + attended
    normed_two = layer_norm(middle, vector_f32[2], vector_f32[3]).astype(jnp.bfloat16)
    hidden = jnp.dot(normed_two, full_up, preferred_element_type=jnp.float32) + up_shift
    active = smooth_gate(hidden).astype(jnp.bfloat16)
    output = middle + (
        jnp.dot(active, full_down, preferred_element_type=jnp.float32) + vector_f32[7]
    )
    again = collect(shard_list)
    full_qkv, full_out, full_up, full_down = (again[0], again[1], again[2], again[3])
    grad_out = cotangent.astype(jnp.float32).reshape(total_tok, D)
    grad_branch = grad_out.astype(jnp.bfloat16)
    grad_down_bias = jnp.sum(grad_branch.astype(jnp.float32), axis=0)
    grad_down = contract_rows(active, grad_branch)
    grad_active = contract_cols(grad_branch, full_down)
    _, gate_back = jax.vjp(smooth_gate, hidden)
    grad_hidden = gate_back(grad_active)[0].astype(jnp.bfloat16)
    grad_up_bias = jnp.sum(grad_hidden.astype(jnp.float32), axis=0)
    grad_up = contract_rows(normed_two, grad_hidden)
    grad_normed_two = contract_cols(grad_hidden, full_up)
    _, norm_two_back = jax.vjp(layer_norm, middle, vector_f32[2], vector_f32[3])
    grad_mid_ln, grad_gain_two, grad_shift_two = norm_two_back(grad_normed_two)
    grad_middle = grad_out + grad_mid_ln
    grad_attended = grad_middle.astype(jnp.bfloat16)
    grad_out_bias = jnp.sum(grad_attended.astype(jnp.float32), axis=0)
    grad_out_w = contract_rows(mixed_flat, grad_attended)
    grad_hidden_bias = grad_up_bias.reshape(4, FF // 4)
    grad_mixed = contract_cols(grad_attended, full_out).astype(jnp.bfloat16)
    grad_packed = lax.map(
        attend_back_row,
        (heads_view, windows, grad_mixed.reshape(row_count, L, HEADS, HD), log_total),
    )
    grad_packed = grad_packed.reshape(total_tok, 3 * D).astype(jnp.bfloat16)
    grad_qkv_bias = jnp.sum(grad_packed.astype(jnp.float32), axis=0)
    grad_qkv = contract_rows(normed_one, grad_packed)
    grad_normed_one = contract_cols(grad_packed, full_qkv)
    grad_table = lax.dot_general(
        flat_onehot,
        grad_normed_one,
        (((0,), (0,)), ((), ())),
        precision=lax.Precision.HIGHEST,
        preferred_element_type=jnp.float32,
    )
    _, norm_one_back = jax.vjp(layer_norm, inputs, vector_f32[0], vector_f32[1])
    grad_in_ln, grad_gain_one, grad_shift_one = norm_one_back(grad_normed_one)
    grad_input = grad_middle + grad_in_ln
    grad_vectors = jnp.stack(
        [
            grad_gain_one,
            grad_shift_one,
            grad_gain_two,
            grad_shift_two,
            grad_qkv_bias[:D],
            grad_qkv_bias[2 * D :],
            grad_out_bias,
            grad_down_bias,
        ],
        axis=0,
    )
    summed = (
        lax.psum_scatter(grad_qkv, "fsdp", scatter_dimension=1, tiled=True),
        lax.psum_scatter(grad_out_w, "fsdp", scatter_dimension=1, tiled=True),
        lax.psum_scatter(grad_up, "fsdp", scatter_dimension=1, tiled=True),
        lax.psum_scatter(grad_down, "fsdp", scatter_dimension=1, tiled=True),
        lax.psum_scatter(grad_vectors, "fsdp", scatter_dimension=1, tiled=True),
        lax.psum_scatter(grad_table, "fsdp", scatter_dimension=1, tiled=True),
        lax.psum_scatter(grad_hidden_bias, "fsdp", scatter_dimension=1, tiled=True),
    )
    shares = (
        lax.psum_scatter(
            summed[0].astype(jnp.bfloat16), "dp", scatter_dimension=0, tiled=True
        ).astype(jnp.float32),
        lax.psum_scatter(
            summed[1].astype(jnp.bfloat16), "dp", scatter_dimension=0, tiled=True
        ).astype(jnp.float32),
        lax.psum_scatter(
            summed[2].astype(jnp.bfloat16), "dp", scatter_dimension=0, tiled=True
        ).astype(jnp.float32),
        lax.psum_scatter(
            summed[3].astype(jnp.bfloat16), "dp", scatter_dimension=0, tiled=True
        ).astype(jnp.float32),
        lax.psum_scatter(
            summed[4].astype(jnp.bfloat16), "dp", scatter_dimension=0, tiled=True
        ).astype(jnp.float32),
        lax.psum_scatter(
            summed[5].astype(jnp.bfloat16), "dp", scatter_dimension=0, tiled=True
        ).astype(jnp.float32),
        lax.psum_scatter(
            summed[6].astype(jnp.bfloat16), "dp", scatter_dimension=0, tiled=True
        ).astype(jnp.float32),
    )
    return (
        output.reshape(row_count, L, D).astype(jnp.bfloat16),
        grad_input.reshape(row_count, L, D),
        shares[0],
        shares[1],
        shares[2],
        shares[3],
        shares[4],
        shares[5],
        shares[6],
    )


def solution(mesh):
    placed = (
        P(("dp", "fsdp"), None, None),
        P(("dp", "fsdp"), None),
        P(("dp", "fsdp"), None),
        P(("dp", "fsdp"), None, None),
        P("dp", "fsdp"),
        P("dp", "fsdp"),
        P("dp", "fsdp"),
        P("dp", "fsdp"),
        P("dp", "fsdp"),
        P("dp", "fsdp"),
        P("dp", "fsdp"),
    )
    return jax.shard_map(
        per_device,
        mesh=mesh,
        in_specs=placed,
        out_specs=(
            P(("dp", "fsdp"), None, None),
            P(("dp", "fsdp"), None, None),
            P("dp", "fsdp"),
            P("dp", "fsdp"),
            P("dp", "fsdp"),
            P("dp", "fsdp"),
            P("dp", "fsdp"),
            P("dp", "fsdp"),
            P("dp", "fsdp"),
        ),
        check_vma=False,
    )
```

profile of v0, /device:TPU:0, one launch (start us, length us, event | category | flops | bytes accessed | tf_op | source)
XLA Modules:
  0.0 1342.2 jit_solution(5047334200031618065)
XLA Ops:
  7.3 9.3 all_gather.54
  17.7 5.8 all_gather.56
  24.4 9.2 all_gather.58
  33.7 8.1 all_gather.62
  42.1 5.0 all-gather
  47.1 5.0 all-gather.4
  53.3 20.9 %all-gather.5 = bf16[8,96,4]{1,2,0:T(4,128)(2,1)S(1)} all-gather(bf16[1,96,4]{1,2,0:T(4,128)(2,1)S(1)} %bitcast.232), channel_id=1, replica_groups=mesh['dp'=4,'fsdp'=8] {'fsdp'}, dimensions={0}, use_global_device_ids=true | all-gather | bytes 6912 | tf_op jit(solution)/shard_map/all_gather | solution.py:71
  74.9 5.1 all-gather.2
  80.1 26.0 %all-gather.1 = bf16[8,96,8]{1,2,0:T(8,128)(2,1)S(1)} all-gather(bf16[1,96,8]{1,2,0:T(8,128)(2,1)S(1)} %bitcast.231), channel_id=1, replica_groups=mesh['dp'=4,'fsdp'=8] {'fsdp'}, dimensions={0}, use_global_device_ids=true | all-gather | bytes 13824 | tf_op jit(solution)/shard_map/all_gather | solution.py:69
  106.8 31.0 %all-gather.3 = bf16[8,96,20]{1,2,0:T(8,128)(2,1)S(1)} all-gather(bf16[1,96,20]{1,2,0:T(8,128)(2,1)S(1)} %bitcast.230), channel_id=1, replica_groups=mesh['dp'=4,'fsdp'=8] {'fsdp'}, dimensions={0}, use_global_device_ids=true | all-gather | bytes 34560 | tf_op jit(solution)/shard_map/all_gather | solution.py:70
  140.4 8.5 add_convert_fusion.1
  148.9 6.6 copy.99
  155.6 4.3 slice_bitcast_fusion
  162.2 3.0 copy.100
  165.2 85.2 %while.45 = (s32[]{:T(128)}, bf16[2,512,12,64]{1,3,2,0:T(8,128)(2,1)S(1)}, f32[2,12,512]{2,1,0:T(8,128)S(1)}, s32[2,512]{1,0:T(2,128)S(1)}, s32[1024]{0:T(1024)S...) while((s32[]{:T(128)}, ...), condition=%wide.region_8.9_spmd, body=%wide.region_5.8_spmd.sunk | while | flops 1686628352 | bytes 184010896 | solution.py:104
  165.6 12.1 fusion.120
  177.6 12.3 fusion.121
  190.0 3.1 copy-done
  193.1 9.0 bitcast_dynamic-update-slice_fusion.4
  202.6 12.0 fusion.120
  214.5 12.6 fusion.121
  227.1 3.5 copy-done
  230.6 9.0 bitcast_dynamic-update-slice_fusion.4
  251.6 3.2 copy.101
  256.3 3.3 fusion.72
  261.9 38.1 %multiply_convert_fusion.1 = (bf16[1024,3072]{1,0:T(8,128)(2,1)}, f32[1024,3072]{1,0:T(8,128)}, f32[1024,3072]{1,0:T(8,128)}) fusion(f32[3072]{0:T(1024)S(1)} %copy-done.43, bf16[768,3072]{1,0:T(8,128)(2,1)} %all-gather.15.cloned.1.call-done, f32[1024,768]{1,0:T(8,128)} %copy-done.2, f32[768]{0:T(1024)S(1)} %copy-done.29, f32[768]{0:T(1024)S(1)} %copy-done.25, ...), kind=kOutput, calls=%fused_computation.48 | convolution fusion | flops 5043388416 | bytes 39348224 | tf_op jit(solution)/shard_map/dot_general | solution.py:192
  300.0 18.4 %convert_reduce_fusion = (f32[3072]{0:T(1024)}, bf16[1024,3072]{1,0:T(8,128)(2,1)}) fusion(f32[1024,3072]{1,0:T(8,128)} %get-tuple-element.436, bf16[3072,768]{0,1:T(8,128)(2,1)} %all-gather.17.cloned.1.call-done, bf16[1,1024,768]{2,1,0:T(8,128)(2,1)S(1)} %copy-done.13, f32[1024,3072]{1,0:T(8,128)} %get-tuple-element.450, f32[3072]{0:T(1024)S(1)} %copy-done.43), kind=kOutput, calls=%fused_computation.46 | convolution fusion | flops 4885312512 | bytes 37773312 | tf_op jit(solution)/shard_map/dot_general | solution.py:49
  318.5 8.7 multiply_reduce_fusion.1
  331.6 2.9 fusion.73
  334.4 3.9 convolution_convert_fusion
  342.5 2.9 copy.107
  345.4 226.0 %while.46 = (s32[]{:T(128)}, f32[1024,12,64]{0,2,1:T(8,128)}, f32[1024,12,64]{0,2,1:T(8,128)}, bf16[2,512,12,64]{1,0,3,2:T(2,128)(2,1)}, bf16[2,512,12,64]{1,3,2...) while((s32[]{:T(128)}, f32[1024,12,64]{0,2,1:T(8,128)}, ...), condition=%wide.region_15.16_spmd.clone, body=%wide.region_13.15_spmd.clone.sunk | while | flops 4126140416 | bytes 224848080 | solution.py:148
  346.0 11.5 fusion.131
  357.5 13.8 %bitcast_add_fusion.5 = f32[1024,12,64]{0,2,1:T(8,128)} fusion(f32[1024,12,64]{0,2,1:T(8,128)} %get-tuple-element.621, f32[12,512,1024]{2,1,0:T(8,128)} %fusion.131, f32[12,512]{1,0:T(8,128)S(1)} %dynamic-slice_bitcast_fusion.2, pred[512,1024]{1,0:T(8,128)(4,1)S(1)} %broadcast_compare_fusion.5, pred[]{:T(512)S(6)} %compare.3, ...), kind=kOutput, calls=%fused_computation.22.clone.1 | convolution fusion | flops 832045056 | bytes 32800772 | tf_op jit(solution)/shard_map/while/body/eval_jaxpr/while/body/eval_jaxpr/hqk,qhd->khd/dot_general | solution.py:142
  371.3 18.3 %multiply_reduce_fusion.5 = (f32[12,512]{1,0:T(8,128)S(1)}, f32[12,512,1024]{2,1,0:T(8,128)}) fusion(f32[12,512,1024]{2,1,0:T(8,128)} %fusion.131, f32[12,512]{1,0:T(8,128)S(1)} %dynamic-slice_bitcast_fusion.2, pred[512,1024]{1,0:T(8,128)(4,1)S(1)} %broadcast_compare_fusion.5, bf16[1024,12,64]{0,2,1:T(8,128)(2,1)} %get-tuple-element.642, ...), kind=kOutput, calls=%fused_computation.17.clone.1 | convolution fusion | flops 836757504 | bytes 53264388 | tf_op jit(solution)/shard_map/while/body/eval_jaxpr/while/body/eval_jaxpr/qhd,khd->hqk/dot_general | solution.py:124
  389.5 21.8 %multiply_convert_fusion.3 = bf16[12,512,1024]{2,1,0:T(8,128)(2,1)} fusion(f32[12,512,1024]{2,1,0:T(8,128)} %get-tuple-element.577, f32[12,512,1024]{2,1,0:T(8,128)} %fusion.131, f32[12,512]{1,0:T(8,128)S(1)} %get-tuple-element.578, f32[12,512]{1,0:T(8,128)S(1)} %dynamic-slice_bitcast_fusion.2, pred[512,1024]{1,0:T(8,128)(4,1)S(1)} %broadcast_compare_fusion.5), kind=kLoop, calls=%fused_computation.16.clone.1 | loop fusion | flops 37748736 | bytes 63488000 | tf_op jit(solution)/shard_map/while/body/eval_jaxpr/while/body/eval_jaxpr/convert_element_type | solution.py:130
  411.4 9.4 multiply_bitcast_fusion.2
  420.7 8.9 bitcast_add_fusion.4
  431.1 26.9 %dynamic_update_slice.28 = bf16[2,512,12,64]{1,0,3,2:T(2,128)(2,1)} dynamic-update-slice(bf16[2,512,12,64]{1,0,3,2:T(2,128)(2,1)} %get-tuple-element.622, bf16[1,512,12,64]{1,0,3,2:T(2,128)(2,1)S(1)} %copy.146, s32[]{:T(128)S(6)} %copy.163, s32[]{:T(128)} %constant.42.clone.1..sunk, s32[]{:T(128)} %constant.42.clone.1..sunk, s32[]{:T(128)} %constant.42.clone.1..sunk) | dynamic-update-slice | bytes 1572868 | tf_op jit(solution)/shard_map/while/body/eval_jaxpr/while/body/jit(dynamic_update_index_in_dim)/dynamic_update_slice | solution.py:104
  458.4 11.4 fusion.131
  469.8 14.3 %bitcast_add_fusion.5 = f32[1024,12,64]{0,2,1:T(8,128)} fusion(f32[1024,12,64]{0,2,1:T(8,128)} %get-tuple-element.621, f32[12,512,1024]{2,1,0:T(8,128)} %fusion.131, f32[12,512]{1,0:T(8,128)S(1)} %dynamic-slice_bitcast_fusion.2, pred[512,1024]{1,0:T(8,128)(4,1)S(1)} %broadcast_compare_fusion.5, pred[]{:T(512)S(6)} %compare.3, ...), kind=kOutput, calls=%fused_computation.22.clone.1 | convolution fusion | flops 832045056 | bytes 32800772 | tf_op jit(solution)/shard_map/while/body/eval_jaxpr/while/body/eval_jaxpr/hqk,qhd->khd/dot_general | solution.py:142
  484.2 18.1 %multiply_reduce_fusion.5 = (f32[12,512]{1,0:T(8,128)S(1)}, f32[12,512,1024]{2,1,0:T(8,128)}) fusion(f32[12,512,1024]{2,1,0:T(8,128)} %fusion.131, f32[12,512]{1,0:T(8,128)S(1)} %dynamic-slice_bitcast_fusion.2, pred[512,1024]{1,0:T(8,128)(4,1)S(1)} %broadcast_compare_fusion.5, bf16[1024,12,64]{0,2,1:T(8,128)(2,1)} %get-tuple-element.642, ...), kind=kOutput, calls=%fused_computation.17.clone.1 | convolution fusion | flops 836757504 | bytes 53264388 | tf_op jit(solution)/shard_map/while/body/eval_jaxpr/while/body/eval_jaxpr/qhd,khd->hqk/dot_general | solution.py:124
  502.2 21.2 %multiply_convert_fusion.3 = bf16[12,512,1024]{2,1,0:T(8,128)(2,1)} fusion(f32[12,512,1024]{2,1,0:T(8,128)} %get-tuple-element.577, f32[12,512,1024]{2,1,0:T(8,128)} %fusion.131, f32[12,512]{1,0:T(8,128)S(1)} %get-tuple-element.578, f32[12,512]{1,0:T(8,128)S(1)} %dynamic-slice_bitcast_fusion.2, pred[512,1024]{1,0:T(8,128)(4,1)S(1)} %broadcast_compare_fusion.5), kind=kLoop, calls=%fused_computation.16.clone.1 | loop fusion | flops 37748736 | bytes 63488000 | tf_op jit(solution)/shard_map/while/body/eval_jaxpr/while/body/eval_jaxpr/convert_element_type | solution.py:130
  523.5 9.4 multiply_bitcast_fusion.2
  532.9 9.8 bitcast_add_fusion.4
  544.1 26.9 %dynamic_update_slice.28 = bf16[2,512,12,64]{1,0,3,2:T(2,128)(2,1)} dynamic-update-slice(bf16[2,512,12,64]{1,0,3,2:T(2,128)(2,1)} %get-tuple-element.622, bf16[1,512,12,64]{1,0,3,2:T(2,128)(2,1)S(1)} %copy.146, s32[]{:T(128)S(6)} %copy.163, s32[]{:T(128)} %constant.42.clone.1..sunk, s32[]{:T(128)} %constant.42.clone.1..sunk, s32[]{:T(128)} %constant.42.clone.1..sunk) | dynamic-update-slice | bytes 1572868 | tf_op jit(solution)/shard_map/while/body/eval_jaxpr/while/body/jit(dynamic_update_index_in_dim)/dynamic_update_slice | solution.py:104
  571.4 3.9 reshape.388
  580.5 5.8 fusion.74
  588.2 10.6 fusion.65
  598.9 10.0 fusion.52
  610.6 8.3 fusion.67
  626.7 5.4 convolution_bitcast_fusion
  634.1 78.9 %reduce-scatter.22.cloned.1.call-done = f32[768,288]{0,1:T(8,128)} async-done(((f32[768,2304]{0,1:T(8,128)}), f32[768,288]{0,1:T(8,128)}) %reduce-scatter.22.cloned.1.call-update) | async-done | bytes 884752 | tf_op jit(solution)/shard_map/reduce_scatter | solution.py:249
  717.2 162.2 %reduce-scatter.26.cloned.1.call-done = f32[768,384]{1,0:T(8,128)} async-done(((f32[768,3072]{1,0:T(8,128)}), f32[768,384]{1,0:T(8,128)}) %reduce-scatter.26.cloned.1.call-update) | async-done | bytes 1179664 | tf_op jit(solution)/shard_map/reduce_scatter | solution.py:251
  883.5 162.4 %reduce-scatter.30.cloned.1.call-done = f32[3072,96]{0,1:T(8,128)} async-done(((f32[3072,768]{0,1:T(8,128)}), f32[3072,96]{0,1:T(8,128)}) %reduce-scatter.30.cloned.1.call-update) | async-done | bytes 1179664 | tf_op jit(solution)/shard_map/reduce_scatter | solution.py:252
  1048.1 9.5 fusion.55
  1057.6 52.5 %reduce-scatter.42.cloned.1.call-done = f32[96,4]{1,0:T(8,128)} async-done(((f32[768,4]{1,0:T(8,128)}), f32[96,4]{1,0:T(8,128)}) %reduce-scatter.42.cloned.1.call-update) | async-done | bytes 1552
  1110.9 63.0 %reduce-scatter.38.cloned.1.call-done = f32[96,8]{1,0:T(8,128)} async-done(((f32[768,8]{1,0:T(8,128)}), f32[96,8]{1,0:T(8,128)}) %reduce-scatter.38.cloned.1.call-update) | async-done | bytes 3088
  1174.8 63.2 %reduce-scatter.40.cloned.1.call-done = f32[96,20]{1,0:T(8,128)} async-done(((f32[768,20]{1,0:T(8,128)}), f32[96,20]{1,0:T(8,128)}) %reduce-scatter.40.cloned.1.call-update) | async-done | bytes 7696
  1238.9 5.9 all-reduce.3
  1247.1 12.7 reduce-scatter.36.cloned.1.call-done
  1261.4 23.1 %reduce-scatter.34.cloned.1.call-done = bf16[192,288]{1,0:T(8,128)(2,1)} async-done(((bf16[768,288]{1,0:T(8,128)(2,1)}), bf16[192,288]{1,0:T(8,128)(2,1)}) %reduce-scatter.34.cloned.1.call-update) | async-done | bytes 110608
  1286.4 22.8 %reduce-scatter.28.cloned.1.call-done = bf16[192,384]{1,0:T(8,128)(2,1)} async-done(((bf16[768,384]{1,0:T(8,128)(2,1)}), bf16[192,384]{1,0:T(8,128)(2,1)}) %reduce-scatter.28.cloned.1.call-update) | async-done | bytes 147472 | tf_op jit(solution)/shard_map/reduce_scatter | solution.py:264
  1310.8 23.0 %reduce-scatter.32.cloned.1.call-done = bf16[768,96]{0,1:T(8,128)(2,1)} async-done(((bf16[3072,96]{0,1:T(8,128)(2,1)}), bf16[768,96]{0,1:T(8,128)(2,1)}) %reduce-scatter.32.cloned.1.call-update) | async-done | bytes 147472 | tf_op jit(solution)/shard_map/reduce_scatter | solution.py:267
  (244 shorter events, 66.4 us)
Async XLA Ops:
  7.2 26.5 %copy-start.24 = (bf16[768,96]{0,1:T(8,128)(2,1)S(1)}, bf16[768,96]{0,1:T(8,128)(2,1)}, u32[]{:S(2)}) copy-start(bf16[768,96]{0,1:T(8,128)(2,1)} %param.22) | copy-start | bytes 442372
  7.2 34.7 %copy-start.54 = (s32[1,8]{1,0:T(1,128)S(1)}, s32[1,8]{1,0:T(1,128)}, u32[]{:S(2)}) copy-start(s32[1,8]{1,0:T(1,128)} %param.16) | copy-start | bytes 100
  7.2 34.9 %copy-start.49 = (bf16[2,96]{1,0:T(2,128)(2,1)S(1)}, bf16[2,96]{1,0:T(2,128)(2,1)}, u32[]{:S(2)}) copy-start(bf16[2,96]{1,0:T(2,128)(2,1)} %param.23) | copy-start | bytes 1156
  7.2 39.9 %copy-start.50 = (bf16[1,96]{1,0:T(2,128)(2,1)S(1)}, bf16[1,96]{1,0:T(2,128)(2,1)}, u32[]{:S(2)}) copy-start(bf16[1,96]{1,0:T(2,128)(2,1)} %param.25) | copy-start | bytes 580
  7.2 45.0 %copy-start.51 = (s32[1,8]{1,0:T(1,128)S(1)}, s32[1,8]{1,0:T(1,128)}, u32[]{:S(2)}) copy-start(s32[1,8]{1,0:T(1,128)} %param.17) | copy-start | bytes 100
  7.2 45.1 %copy-start.8 = (bf16[1,1024,768]{2,1,0:T(8,128)(2,1)S(1)}, bf16[1,1024,768]{2,1,0:T(8,128)(2,1)}, u32[]{:S(2)}) copy-start(bf16[1,1024,768]{2,1,0:T(8,128)(2,1)} %param.15) | copy-start | bytes 4718596
  7.2 133.2 %all-gather.11.cloned.1.call-start = ((), (), s32[]{:S(2)}) async-start(), calls=%async_computation.11 | async-start | bytes 3981312 | tf_op jit(solution)/shard_map/all_gather | solution.py:65
  17.6 238.7 %all-gather.13.cloned.1.call-start = ((), (), s32[]{:S(2)}) async-start(), calls=%async_computation.12 | async-start | bytes 1327104 | tf_op jit(solution)/shard_map/all_gather | solution.py:66
  24.3 50.6 %copy-start.48 = (bf16[5,96]{1,0:T(8,128)(2,1)S(1)}, bf16[5,96]{1,0:T(8,128)(2,1)}, u32[]{:S(2)}) copy-start(bf16[5,96]{1,0:T(8,128)(2,1)} %param.24) | copy-start | bytes 2884
  24.3 237.6 %all-gather.15.cloned.1.call-start = ((), (), s32[]{:S(2)}) async-start(), calls=%async_computation.13 | async-start | bytes 5308416 | tf_op jit(solution)/shard_map/all_gather | solution.py:67
  33.6 266.4 %all-gather.17.cloned.1.call-start = ((), (), s32[]{:S(2)}) async-start(), calls=%async_computation.14 | async-start | bytes 5308416 | tf_op jit(solution)/shard_map/all_gather | solution.py:68
  41.8 590.4 %reduce-scatter.24.cloned.1.call-start = ((), (), s32[]{:S(2)}) async-start(), calls=%async_computation.16 | async-start | bytes 2654208 | tf_op jit(solution)/shard_map/reduce_scatter | solution.py:250
  52.4 88.0 %copy-start.40 = (s32[1024]{0:T(1024)}, s32[1024]{0:T(1024)S(1)}, u32[]{:S(2)}) copy-start(s32[1024]{0:T(1024)S(1)} %compare_select_fusion) | copy-start | bytes 12292
  52.7 87.7 %copy-start.27 = (f32[1024]{0:T(1024)}, f32[1024]{0:T(1024)S(1)}, u32[]{:S(2)}) copy-start(f32[1024]{0:T(1024)S(1)} %broadcast_multiply_fusion.1) | copy-start | bytes 12292
  53.3 52.9 %copy-start.37 = (f32[1024]{0:T(1024)}, f32[1024]{0:T(1024)S(1)}, u32[]{:S(2)}) copy-start(f32[1024]{0:T(1024)S(1)} %fusion.49) | copy-start | bytes 12292
  53.3 95.6 %copy-start.33 = (f32[1024]{0:T(1024)}, f32[1024]{0:T(1024)S(1)}, u32[]{:S(2)}) copy-start(f32[1024]{0:T(1024)S(1)} %fusion.58) | copy-start | bytes 12292
  106.8 42.1 %copy-start.31 = (f32[768]{0:T(1024)}, f32[768]{0:T(1024)S(1)}, u32[]{:S(2)}) copy-start(f32[768]{0:T(1024)S(1)} %get-tuple-element.387) | copy-start | bytes 9220
  162.2 3.0 copy-start.16
  177.6 15.5 %copy-start = (f32[12,512,1024]{2,1,0:T(8,128)S(1)}, f32[12,512,1024]{2,1,0:T(8,128)}, u32[]{:S(2)}) copy-start(f32[12,512,1024]{2,1,0:T(8,128)} %get-tuple-element.564) | copy-start | bytes 75497472 | tf_op jit(solution)/shard_map/while/body/eval_jaxpr/while
  214.5 16.1 %copy-start = (f32[12,512,1024]{2,1,0:T(8,128)S(1)}, f32[12,512,1024]{2,1,0:T(8,128)}, u32[]{:S(2)}) copy-start(f32[12,512,1024]{2,1,0:T(8,128)} %get-tuple-element.564) | copy-start | bytes 75497472 | tf_op jit(solution)/shard_map/while/body/eval_jaxpr/while
  251.6 4.7 copy-start.9
  251.6 4.7 copy-start.45
  259.7 2.2 copy-start.25
  259.7 2.2 copy-start.29
  259.7 2.2 copy-start.43
  259.7 67.5 %copy-start.20 = (f32[1024]{0:T(1024)}, f32[1024]{0:T(1024)S(1)}, u32[]{:S(2)}) copy-start(f32[1024]{0:T(1024)S(1)} %broadcast_multiply_fusion) | copy-start | bytes 12292
  261.9 65.4 %copy-start.22 = (f32[1024]{0:T(1024)}, f32[1024]{0:T(1024)S(1)}, u32[]{:S(2)}) copy-start(f32[1024]{0:T(1024)S(1)} %fusion.59) | copy-start | bytes 12292
  261.9 38.1 %copy-start.13 = (bf16[1,1024,768]{2,1,0:T(8,128)(2,1)S(1)}, bf16[1,1024,768]{2,1,0:T(8,128)(2,1)}, u32[]{:S(2)}) copy-start(bf16[1,1024,768]{2,1,0:T(8,128)(2,1)} %param.18) | copy-start | bytes 4718596
  300.0 18.4 %copy-start.3 = (f32[1024,768]{1,0:T(8,128)S(1)}, f32[1024,768]{1,0:T(8,128)}, u32[]{:S(2)}) copy-start(f32[1024,768]{1,0:T(8,128)} %copy-done.2) | copy-start | bytes 9437188
  300.0 18.4 %copy-start.52 = (bf16[768,3072]{1,0:T(8,128)(2,1)S(1)}, bf16[768,3072]{1,0:T(8,128)(2,1)}, u32[]{:S(2)}) copy-start(bf16[768,3072]{1,0:T(8,128)(2,1)} %all-gather.15.cloned.1.call-done) | copy-start | bytes 14155780
  328.8 2.8 copy-start.18
  331.6 2.9 copy-start.53
  345.4 367.7 %reduce-scatter.22.cloned.1.call-start = ((), (), s32[]{:S(2)}) async-start(), calls=%async_computation.15 | async-start | bytes 7962624 | tf_op jit(solution)/shard_map/reduce_scatter | solution.py:249
  346.0 11.5 copy-start.12
  420.7 8.9 copy-start.11
  458.4 11.4 copy-start.12
  532.9 9.8 copy-start.11
  571.4 4.0 copy-start.1
  575.4 5.1 copy-start.56
  578.2 2.3 copy-start.15
  586.3 1.9 copy-start.23
  586.3 1.9 copy-start.26
  586.3 293.1 %reduce-scatter.26.cloned.1.call-start = ((), (), s32[]{:S(2)}) async-start(), calls=%async_computation.17 | async-start | bytes 10616832 | tf_op jit(solution)/shard_map/reduce_scatter | solution.py:251
  598.8 447.0 %reduce-scatter.30.cloned.1.call-start = ((), (), s32[]{:S(2)}) async-start(), calls=%async_computation.19 | async-start | bytes 10616832 | tf_op jit(solution)/shard_map/reduce_scatter | solution.py:252
  608.9 501.1 %reduce-scatter.42.cloned.1.call-start = ((), (), s32[]{:S(2)}) async-start(), calls=%async_computation.25 | async-start | bytes 442368
  610.5 8.4 copy-start.38
  610.5 8.4 copy-start.10
  610.6 8.4 copy-start.34
  618.9 6.5 copy-start.5
  618.9 3.1 copy-start.7
  618.9 3.6 copy-start.14
  618.9 3.6 copy-start.36
  622.5 2.9 copy-start.47
  622.5 2.9 copy-start.46
  622.5 2.9 copy-start.39
  622.5 4.2 copy-start.41
  625.4 548.5 %reduce-scatter.38.cloned.1.call-start = ((), (), s32[]{:S(2)}) async-start(), calls=%async_computation.23 | async-start | bytes 442368
  626.7 611.3 %reduce-scatter.40.cloned.1.call-start = ((), (), s32[]{:S(2)}) async-start(), calls=%async_computation.24 | async-start | bytes 442368
  632.2 249.5 %copy-start.55 = (u32[32]{0:T(128)S(1)}, u32[32]{0:T(128)}, u32[]{:S(2)}) copy-start(u32[32]{0:T(128)} %constant.172) | copy-start | bytes 388
  632.2 627.6 %reduce-scatter.36.cloned.1.call-start = ((), (), s32[]{:S(2)}) async-start(), calls=%async_computation.22 | async-start | bytes 245760
  634.1 650.5 %reduce-scatter.34.cloned.1.call-start = ((), (), s32[]{:S(2)}) async-start(), calls=%async_computation.21 | async-start | bytes 737280
  715.0 333.1 %copy-start.44 = (f32[768]{0:T(1024)S(1)}, f32[768]{0:T(1024)}, u32[]{:S(2)}) copy-start(f32[768]{0:T(1024)} %get-tuple-element.381) | copy-start | bytes 9220
  717.1 592.1 %reduce-scatter.28.cloned.1.call-start = ((), (), s32[]{:S(2)}) async-start(), calls=%async_computation.18 | async-start | bytes 737280 | tf_op jit(solution)/shard_map/reduce_scatter | solution.py:264
  881.6 452.2 %reduce-scatter.32.cloned.1.call-start = ((), (), s32[]{:S(2)}) async-start(), calls=%async_computation.20 | async-start | bytes 737280 | tf_op jit(solution)/shard_map/reduce_scatter | solution.py:267
  (11 other events, 17.1 us)
Sparse Core Ops, SparseCore 0:
  17.7 66.2 all-gather.10
  86.8 39.7 all-gather.12
  128.6 79.9 all-gather.14
  210.6 78.1 all-gather.16
  345.5 66.1 reduce-scatter.23
  586.5 126.5 reduce-scatter.21
  717.0 162.3 reduce-scatter.25
  883.4 162.4 reduce-scatter.29
  1049.5 60.4 reduce-scatter.41
  1113.5 60.3 reduce-scatter.37
  1177.5 60.4 reduce-scatter.39
  1241.0 18.7 reduce-scatter.35
  1262.4 22.0 reduce-scatter.33
  1287.1 22.0 reduce-scatter.27
  1311.7 22.0 reduce-scatter.31
where the time goes:
time: 1350 us; the launch traced here: 1340 us
  waiting for transfers between devices  664 us (49%)
  matrix products  303 us (22%)
  blocking collectives  131 us (10%)
  local copies, waits for them, and re-layouts  121 us (9%)
  other arithmetic  94.8 us (7%)
  between operations  16.2 us (1%)
    unnamed x20, waiting for transfers between devices  215 us
    reduce_scatter x1, waiting for transfers between devices, per_device(): lax.psum_scatter(grad_down, 'fsdp', scatter_dimension=1, tiled=True)  162 us
    reduce_scatter x1, waiting for transfers between devices, per_device(): lax.psum_scatter(grad_up, 'fsdp', scatter_dimension=1, tiled=True)  162 us
    reduce_scatter x1, waiting for transfers between devices, per_device(): lax.psum_scatter(grad_qkv, 'fsdp', scatter_dimension=1, tiled=True)  78.9 us
    dynamic_update_slice x4, local copies, waits for them, and re-layouts, attend_row(): mixture, log_total = lax.map(attend_block, (query_blocks, window_blocks))  56.7 us
    dot_general x4, matrix products, masked_scores(): jnp.einsum('qhd,khd->hqk', query_block, key_heads, preferred_element_type...  46.9 us
    convert_element_type x2, other arithmetic, back_block(): grad_scores = grad_scores.astype(jnp.bfloat16)  43.1 us
    dot_general x4, matrix products, contract_cols(): lax.dot_general(left_side, right_side, (((1,), (1,)), ((), ())), preferre...  39.4 us
  transfers between devices with their start and end apart: 15, of which 10 were waited for; matrix products, arithmetic and copies ran while one was open for 34% of the time, Pallas kernels for 0%

commit v1 on v0

v1 whole, which is shorter than its diff:
```python
import functools

import jax
import jax.numpy as jnp
from jax import lax
from jax.experimental import pallas as pl
from jax.experimental.pallas import tpu as pltpu
from jax.sharding import PartitionSpec as P

D = 768
HEADS = 12
HD = 64
FF = 3072
LEADS = 20
WIN = 8
L = 1024
EPSILON = 1e-05
MASKED = -1e30
ROWS = 256
TILES = L // ROWS
BLK = 128
PAIRS = HEADS // 2
SCALE = HD ** (-0.5)
VMEM_BYTES = 56 * 1024 * 1024

F32 = jnp.float32
BF16 = jnp.bfloat16


def params(limit=VMEM_BYTES):
    return pltpu.CompilerParams(vmem_limit_bytes=limit)


def dot_nn(a, b):
    return lax.dot_general(a, b, (((1,), (0,)), ((), ())), preferred_element_type=F32)


def dot_nt(a, b):
    return lax.dot_general(a, b, (((1,), (1,)), ((), ())), preferred_element_type=F32)


def whole(shape, space=pltpu.VMEM):
    return pl.BlockSpec(shape, lambda *_: (0,) * len(shape), memory_space=space)


def smem():
    return pl.BlockSpec(memory_space=pltpu.SMEM)


def rows_of(width):
    return pl.BlockSpec((ROWS, width), lambda i: (i, 0))


def norm_parts(values):
    center = values - jnp.mean(values, axis=-1, keepdims=True)
    spread = jnp.mean(center * center, axis=-1, keepdims=True)
    inv = lax.rsqrt(spread + EPSILON)
    return center * inv, inv


def bounds_of(lengths_ref):
    found, total = [], 0
    for w in range(WIN):
        total = total + lengths_ref[0, w]
        found.append(total)
    return found


def lead_of(places, bounds, lead_ref):
    lead = jnp.full(places.shape, -1, jnp.int32)
    for w in reversed(range(WIN)):
        lead = jnp.where(places < bounds[w], lead_ref[0, w], lead)
    return lead


def qkv_kernel(len_ref, lead_ref, x_ref, vec_ref, table_ref, w_ref, n1_ref, qkv_ref):
    step = pl.program_id(0)
    bounds = bounds_of(len_ref)
    hat, _ = norm_parts(x_ref[...].astype(F32))
    normed = hat * (1.0 + vec_ref[0:1, :]) + vec_ref[1:2, :]
    shape = (ROWS, table_ref.shape[0])
    places = step * ROWS + lax.broadcasted_iota(jnp.int32, shape, 0)
    hot = lead_of(places, bounds, lead_ref) == lax.broadcasted_iota(jnp.int32, shape, 1)
    n1 = (normed + dot_nn(hot.astype(BF16), table_ref[...])).astype(BF16)
    n1_ref[...] = n1
    for third in range(3):
        cols = slice(third * D, (third + 1) * D)
        part = dot_nn(n1, w_ref[:, cols])
        if third == 0:
            part = (part + vec_ref[4:5, :]).astype(BF16) * jnp.asarray(SCALE, BF16)
        elif third == 2:
            part = part + vec_ref[5:6, :]
        qkv_ref[:, cols] = part.astype(BF16)


def qkv_call(lengths, leads, x, vec, table, w):
    return pl.pallas_call(
        qkv_kernel,
        grid=(TILES,),
        in_specs=[smem(), smem(), rows_of(D), whole(vec.shape), whole(table.shape), whole(w.shape)],
        out_specs=[rows_of(D), rows_of(3 * D)],
        out_shape=[jax.ShapeDtypeStruct((L, D), BF16), jax.ShapeDtypeStruct((L, 3 * D), BF16)],
        compiler_params=params(),
        cost_estimate=pl.CostEstimate(flops=2 * L * D * 3 * D, bytes_accessed=12_000_000, transcendentals=0),
        name="norm_qkv",
    )(lengths, leads, x, vec, table, w)


def block_range(bounds, block):
    first, last = block * BLK, block * BLK + BLK - 1
    start, end = jnp.int32(0), jnp.int32(L)
    for w in range(WIN):
        start = jnp.where(bounds[w] <= first, bounds[w], start)
    for w in reversed(range(WIN)):
        end = jnp.where(bounds[w] > last, bounds[w], end)
    return start // BLK, (end + BLK - 1) // BLK


def window_at(places, bounds):
    found = jnp.zeros(places.shape, jnp.int32)
    for w in range(WIN):
        found = found + (places >= bounds[w]).astype(jnp.int32)
    return found


def hide(bounds, key_block, query_block):
    shape = (BLK, BLK)
    keys = window_at(key_block * BLK + lax.broadcasted_iota(jnp.int32, (BLK, 1), 0), bounds)
    queries = window_at(query_block * BLK + lax.broadcasted_iota(jnp.int32, (1, BLK), 1), bounds)
    one = jnp.where(jnp.broadcast_to(keys, shape) == jnp.broadcast_to(queries, shape), 0.0, MASKED)
    return jnp.concatenate([one, one], axis=1)


def split_pair(two):
    lanes = lax.broadcasted_iota(jnp.int32, two.shape, 1)
    zero = jnp.zeros_like(two)
    return jnp.concatenate([jnp.where(lanes < HD, two, zero), jnp.where(lanes < HD, zero, two)], axis=0)


def attend_kernel(len_ref, qkv_ref, o_ref, lse_ref, vt, qm, acc, top, tot):
    bounds = bounds_of(len_ref)
    for p in range(PAIRS):
        vt[p * BLK:(p + 1) * BLK, :] = qkv_ref[:, 2 * D + p * BLK:2 * D + (p + 1) * BLK].T
    lse_ref[HEADS:, :] = jnp.zeros((lse_ref.shape[0] - HEADS, L), F32)

    def query_step(block, carry):
        at = pl.multiple_of(block * BLK, BLK)
        first, last = block_range(bounds, block)
        for p in range(PAIRS):
            qm[p] = split_pair(qkv_ref[pl.ds(at, BLK), p * BLK:(p + 1) * BLK])
        acc[...] = jnp.zeros_like(acc)
        top[...] = jnp.full_like(top, MASKED)
        tot[...] = jnp.zeros_like(tot)

        def key_step(key_block, carry):
            key_at = pl.multiple_of(key_block * BLK, BLK)
            hidden = hide(bounds, key_block, block)
            for p in range(PAIRS):
                keys = qkv_ref[pl.ds(key_at, BLK), D + p * BLK:D + (p + 1) * BLK]
                scores = dot_nt(keys, qm[p]) + hidden
                old = top[p, 0:1, :]
                new = jnp.maximum(old, jnp.max(scores, axis=0, keepdims=True))
                expo = jnp.exp(scores - new)
                fade = jnp.exp(old - new)
                top[p, 0:1, :] = new
                tot[p, 0:1, :] = tot[p, 0:1, :] * fade + jnp.sum(expo, axis=0, keepdims=True)
                soft = expo.astype(BF16)
                for side in range(2):
                    rows = slice(side * HD, (side + 1) * HD)
                    cols = slice(side * BLK, (side + 1) * BLK)
                    vals = vt[p * BLK + side * HD:p * BLK + (side + 1) * HD, pl.ds(key_at, BLK)]
                    acc[p, rows, :] = acc[p, rows, :] * fade[:, cols] + dot_nn(vals, soft[:, cols])
            return carry

        lax.fori_loop(first, last, key_step, 0)
        for p in range(PAIRS):
            total = tot[p, 0:1, :]
            inv = 1.0 / total
            log_total = top[p, 0:1, :] + jnp.log(total)
            mixed = jnp.concatenate([acc[p, :HD, :] * inv[:, :BLK], acc[p, HD:, :] * inv[:, BLK:]], axis=0)
            o_ref[pl.ds(at, BLK), p * BLK:(p + 1) * BLK] = mixed.T.astype(BF16)
            lse_ref[2 * p:2 * p + 1, pl.ds(at, BLK)] = log_total[:, :BLK]
            lse_ref[2 * p + 1:2 * p + 2, pl.ds(at, BLK)] = log_total[:, BLK:]
        return carry

    lax.fori_loop(0, L // BLK, query_step, 0)


def attend_call(lengths, qkv):
    return pl.pallas_call(
        attend_kernel,
        in_specs=[smem(), pl.BlockSpec(memory_space=pltpu.VMEM)],
        out_specs=[pl.BlockSpec(memory_space=pltpu.VMEM)] * 2,
        out_shape=[jax.ShapeDtypeStruct((L, D), BF16), jax.ShapeDtypeStruct((16, L), F32)],
        scratch_shapes=[
            pltpu.VMEM((D, L), BF16),
            pltpu.VMEM((PAIRS, 2 * BLK, BLK), BF16),
            pltpu.VMEM((PAIRS, BLK, BLK), F32),
            pltpu.VMEM((PAIRS, 8, 2 * BLK), F32),
            pltpu.VMEM((PAIRS, 8, 2 * BLK), F32),
        ],
        compiler_params=params(),
        cost_estimate=pl.CostEstimate(flops=4 * L * L * D, bytes_accessed=8_000_000, transcendentals=0),
        name="attend",
    )(lengths, qkv)


def attend_back_kernel(len_ref, qkv_ref, o_ref, go_ref, lse_ref, g_ref, sums_ref, kt, qm, gm, stat, dq, dk, dv):
    bounds = bounds_of(len_ref)
    for p in range(PAIRS):
        kt[p * BLK:(p + 1) * BLK, :] = qkv_ref[:, D + p * BLK:D + (p + 1) * BLK].T
    dk[...] = jnp.zeros_like(dk)
    dv[...] = jnp.zeros_like(dv)
    sums_ref[...] = jnp.zeros_like(sums_ref)

    def query_step(block, carry):
        at = pl.multiple_of(block * BLK, BLK)
        first, last = block_range(bounds, block)
        for p in range(PAIRS):
            cols = slice(p * BLK, (p + 1) * BLK)
            qm[p] = split_pair(qkv_ref[pl.ds(at, BLK), cols])
            grads = go_ref[pl.ds(at, BLK), cols]
            gm[p] = split_pair(grads)
            prod = (grads.astype(F32) * o_ref[pl.ds(at, BLK), cols].astype(F32)).T
            stat[p, 0:1, :BLK] = lse_ref[2 * p:2 * p + 1, pl.ds(at, BLK)]
            stat[p, 0:1, BLK:] = lse_ref[2 * p + 1:2 * p + 2, pl.ds(at, BLK)]
            stat[p, 1:2, :BLK] = jnp.sum(prod[:HD], axis=0, keepdims=True)
            stat[p, 1:2, BLK:] = jnp.sum(prod[HD:], axis=0, keepdims=True)
        dq[...] = jnp.zeros_like(dq)

        def key_step(key_block, carry):
            key_at = pl.multiple_of(key_block * BLK, BLK)
            hidden = hide(bounds, key_block, block)
            for p in range(PAIRS):
                cols = slice(p * BLK, (p + 1) * BLK)
                keys = qkv_ref[pl.ds(key_at, BLK), D + p * BLK:D + (p + 1) * BLK]
                vals = qkv_ref[pl.ds(key_at, BLK), 2 * D + p * BLK:2 * D + (p + 1) * BLK]
                soft = jnp.exp(dot_nt(keys, qm[p]) + (hidden - stat[p, 0:1, :]))
                grad_soft = dot_nt(vals, gm[p])
                grad_scores = (soft * (grad_soft - stat[p, 1:2, :])).astype(BF16)
                dv[pl.ds(key_at, BLK), cols] += dot_nn(soft.astype(BF16), gm[p])
                dk[pl.ds(key_at, BLK), cols] += dot_nn(grad_scores, qm[p])
                for side in range(2):
                    rows = slice(side * HD, (side + 1) * HD)
                    kside = kt[p * BLK + side * HD:p * BLK + (side + 1) * HD, pl.ds(key_at, BLK)]
                    dq[p, rows, :] += dot_nn(kside, grad_scores[:, side * BLK:(side + 1) * BLK])
            return carry

        lax.fori_loop(first, last, key_step, 0)
        for p in range(PAIRS):
            cols = slice(p * BLK, (p + 1) * BLK)
            done = (dq[p] * SCALE).T.astype(BF16)
            g_ref[pl.ds(at, BLK), cols] = done
            sums_ref[0:1, cols] += jnp.sum(done.astype(F32), axis=0, keepdims=True)
        return carry

    lax.fori_loop(0, L // BLK, query_step, 0)
    g_ref[:, D:2 * D] = dk[...].astype(BF16)
    gv = dv[...].astype(BF16)
    g_ref[:, 2 * D:] = gv
    sums_ref[1:2, :] = jnp.sum(gv.astype(F32), axis=0, keepdims=True)


def attend_back_call(lengths, qkv, o, go, lse):
    return pl.pallas_call(
        attend_back_kernel,
        in_specs=[smem()] + [pl.BlockSpec(memory_space=pltpu.VMEM)] * 4,
        out_specs=[pl.BlockSpec(memory_space=pltpu.VMEM)] * 2,
        out_shape=[jax.ShapeDtypeStruct((L, 3 * D), BF16), jax.ShapeDtypeStruct((8, D), F32)],
        scratch_shapes=[
            pltpu.VMEM((D, L), BF16),
            pltpu.VMEM((PAIRS, 2 * BLK, BLK), BF16),
            pltpu.VMEM((PAIRS, 2 * BLK, BLK), BF16),
            pltpu.VMEM((PAIRS, 8, 2 * BLK), F32),
            pltpu.VMEM((PAIRS, BLK, BLK), F32),
            pltpu.VMEM((L, D), F32),
            pltpu.VMEM((L, D), F32),
        ],
        compiler_params=params(),
        cost_estimate=pl.CostEstimate(flops=10 * L * L * D, bytes_accessed=15_000_000, transcendentals=0),
        name="attend_back",
    )(lengths, qkv, o, go, lse)


def gate_pair(h):
    size = jnp.abs(h)
    t = 1.0 / (1.0 + (0.3275911 * 0.7071067811865476) * size)
    bell = jnp.exp(-0.5 * h * h)
    poly = t * (0.127414796 + t * (-0.142248368 + t * (0.7107068705 + t * (-0.7265760135 + t * 0.5307027145))))
    tail = poly * bell
    cdf = jnp.where(h >= 0.0, 1.0 - tail, tail)
    return h * cdf, cdf + h * (0.3989422804014327 * bell)


def up_kernel(o_ref, x_ref, vec_ref, wo_ref, wu_ref, bu_ref, mid_ref, n2_ref, a_ref, slope_ref):
    middle = x_ref[...].astype(F32) + (dot_nn(o_ref[...], wo_ref[...]) + vec_ref[6:7, :])
    mid_ref[...] = middle
    hat, _ = norm_parts(middle)
    n2 = (hat * (1.0 + vec_ref[2:3, :]) + vec_ref[3:4, :]).astype(BF16)
    n2_ref[...] = n2
    width = 512
    for c in range(FF // width):
        cols = slice(c * width, (c + 1) * width)
        h = dot_nn(n2, wu_ref[:, cols]) + bu_ref[:, cols]
        act, slope = gate_pair(h)
        a_ref[:, cols] = act.astype(BF16)
        slope_ref[:, cols] = slope.astype(BF16)


def up_call(o, x, vec, wo, wu, bu):
    return pl.pallas_call(
        up_kernel,
        grid=(TILES,),
        in_specs=[rows_of(D), rows_of(D), whole(vec.shape), whole(wo.shape), whole(wu.shape), whole(bu.shape)],
        out_specs=[rows_of(D), rows_of(D), rows_of(FF), rows_of(FF)],
        out_shape=[
            jax.ShapeDtypeStruct((L, D), F32),
            jax.ShapeDtypeStruct((L, D), BF16),
            jax.ShapeDtypeStruct((L, FF), BF16),
            jax.ShapeDtypeStruct((L, FF), BF16),
        ],
        compiler_params=params(),
        cost_estimate=pl.CostEstimate(flops=2 * L * D * (FF + D), bytes_accessed=25_000_000, transcendentals=2 * L * FF),
        name="feed_up",
    )(o, x, vec, wo, wu, bu)


def down_kernel(a_ref, mid_ref, vec_ref, wdt_ref, y_ref):
    y_ref[...] = (mid_ref[...] + (dot_nt(a_ref[...], wdt_ref[...]) + vec_ref[7:8, :])).astype(BF16)


def down_call(a, middle, vec, wdt):
    return pl.pallas_call(
        down_kernel,
        grid=(TILES,),
        in_specs=[rows_of(FF), rows_of(D), whole(vec.shape), whole(wdt.shape)],
        out_specs=rows_of(D),
        out_shape=jax.ShapeDtypeStruct((L, D), BF16),
        compiler_params=params(),
        cost_estimate=pl.CostEstimate(flops=2 * L * D * FF, bytes_accessed=17_000_000, transcendentals=0),
        name="feed_down",
    )(a, middle, vec, wdt)


def norm_back(grad, hat, inv, gain):
    scaled = grad * (1.0 + gain)
    both = jnp.mean(scaled * hat, axis=-1, keepdims=True)
    return inv * (scaled - jnp.mean(scaled, axis=-1, keepdims=True) - hat * both)


def feed_back_kernel(gy_ref, slope_ref, mid_ref, vec_ref, wdt_ref, wu_ref, wo_ref,
                     gh_ref, gmid_ref, gatt_ref, go_ref, sums_ref, bup_ref):
    @pl.when(pl.program_id(0) == 0)
    def _():
        sums_ref[...] = jnp.zeros_like(sums_ref)
        bup_ref[...] = jnp.zeros_like(bup_ref)

    gm = gy_ref[...]
    gy = gm.astype(F32)
    width = 768
    gn2 = None
    for c in range(FF // width):
        cols = slice(c * width, (c + 1) * width)
        ga = dot_nn(gm, wdt_ref[:, cols])
        gh = (ga * slope_ref[:, cols].astype(F32)).astype(BF16)
        gh_ref[:, cols] = gh
        bup_ref[0:1, cols] += jnp.sum(gh.astype(F32), axis=0, keepdims=True)
        part = dot_nt(gh, wu_ref[:, cols])
        gn2 = part if gn2 is None else gn2 + part
    hat, inv = norm_parts(mid_ref[...])
    sums_ref[0:1, :] += jnp.sum(gn2 * hat, axis=0, keepdims=True)
    sums_ref[1:2, :] += jnp.sum(gn2, axis=0, keepdims=True)
    gmid = gy + norm_back(gn2, hat, inv, vec_ref[2:3, :])
    gmid_ref[...] = gmid
    gatt = gmid.astype(BF16)
    gatt_ref[...] = gatt
    sums_ref[2:3, :] += jnp.sum(gatt.astype(F32), axis=0, keepdims=True)
    sums_ref[3:4, :] += jnp.sum(gy, axis=0, keepdims=True)
    go_ref[...] = dot_nt(gatt, wo_ref[...]).astype(BF16)


def feed_back_call(gy, slope, middle, vec, wdt, wu, wo):
    return pl.pallas_call(
        feed_back_kernel,
        grid=(TILES,),
        in_specs=[rows_of(D), rows_of(FF), rows_of(D), whole(vec.shape), whole(wdt.shape), whole(wu.shape), whole(wo.shape)],
        out_specs=[rows_of(FF), rows_of(D), rows_of(D), rows_of(D), whole((8, D)), whole((8, FF))],
        out_shape=[
            jax.ShapeDtypeStruct((L, FF), BF16),
            jax.ShapeDtypeStruct((L, D), F32),
            jax.ShapeDtypeStruct((L, D), BF16),
            jax.ShapeDtypeStruct((L, D), BF16),
            jax.ShapeDtypeStruct((8, D), F32),
            jax.ShapeDtypeStruct((8, FF), F32),
        ],
        compiler_params=params(),
        cost_estimate=pl.CostEstimate(flops=2 * L * D * (2 * FF + D), bytes_accessed=35_000_000, transcendentals=0),
        name="feed_back",
    )(gy, slope, middle, vec, wdt, wu, wo)


def outer_kernel(left_ref, right_ref, out_ref, turned):
    @pl.when(pl.program_id(0) == 0)
    def _():
        turned[...] = left_ref[...].T

    out_ref[...] = dot_nn(turned[...], right_ref[...]).astype(BF16)


def outer_call(left, right, name):
    wide = right.shape[1]
    width = 768
    return pl.pallas_call(
        outer_kernel,
        grid=(wide // width,),
        in_specs=[whole(left.shape), pl.BlockSpec((L, width), lambda i: (0, i))],
        out_specs=pl.BlockSpec((D, width), lambda i: (0, i)),
        out_shape=jax.ShapeDtypeStruct((D, wide), BF16),
        scratch_shapes=[pltpu.VMEM((D, L), BF16)],
        compiler_params=params(),
        cost_estimate=pl.CostEstimate(flops=2 * L * D * wide, bytes_accessed=4 * L * D + 4 * D * wide, transcendentals=0),
        name=name,
    )(left, right)


def first_back_kernel(len_ref, lead_ref, x_ref, gmid_ref, g_ref, vec_ref, w_ref, out_ref, sums_ref, table_ref):
    step = pl.program_id(0)

    @pl.when(step == 0)
    def _():
        sums_ref[...] = jnp.zeros_like(sums_ref)
        table_ref[...] = jnp.zeros_like(table_ref)

    gn1 = dot_nt(g_ref[...], w_ref[...])
    hat, inv = norm_parts(x_ref[...].astype(F32))
    sums_ref[0:1, :] += jnp.sum(gn1 * hat, axis=0, keepdims=True)
    sums_ref[1:2, :] += jnp.sum(gn1, axis=0, keepdims=True)
    shape = (table_ref.shape[0], ROWS)
    places = step * ROWS + lax.broadcasted_iota(jnp.int32, shape, 1)
    hot = lead_of(places, bounds_of(len_ref), lead_ref) == lax.broadcasted_iota(jnp.int32, shape, 0)
    hot = hot.astype(BF16)
    high = gn1.astype(BF16)
    low = (gn1 - high.astype(F32)).astype(BF16)
    table_ref[...] += dot_nn(hot, high) + dot_nn(hot, low)
    out_ref[...] = gmid_ref[...] + norm_back(gn1, hat, inv, vec_ref[0:1, :])


def first_back_call(lengths, leads, x, gmid, gqkv, vec, w):
    return pl.pallas_call(
        first_back_kernel,
        grid=(TILES,),
        in_specs=[smem(), smem(), rows_of(D), rows_of(D), rows_of(3 * D), whole(vec.shape), whole(w.shape)],
        out_specs=[rows_of(D), whole((8, D)), whole((32, D))],
        out_shape=[
            jax.ShapeDtypeStruct((L, D), F32),
            jax.ShapeDtypeStruct((8, D), F32),
            jax.ShapeDtypeStruct((32, D), F32),
        ],
        compiler_params=params(),
        cost_estimate=pl.CostEstimate(flops=2 * L * D * 3 * D, bytes_accessed=17_000_000, transcendentals=0),
        name="first_back",
    )(lengths, leads, x, gmid, gqkv, vec, w)


def hop_dp(value, flip, ranks):
    return lax.ppermute(value, "dp", [(i, i ^ flip) for i in range(ranks)])


def hop_fsdp(value, flip, ranks):
    return lax.ppermute(value, "fsdp", [(i, i ^ flip) for i in range(ranks)])


def after(value, *others):
    return lax.optimization_barrier((value,) + others)[0]


def gather_shards(piece, sizes):
    dps, fss = sizes
    deep = fss // 2
    along = [piece] + [hop_fsdp(piece, 2 * z, fss) for z in range(1, deep)]
    half = max(deep // 2, 1)
    first, second = jnp.stack(along[:half]), jnp.stack(along[half:])
    by_x = [hop_dp(first, 2, dps), hop_dp(second, 2, dps)]
    by_y = [hop_fsdp(first, 1, fss), hop_fsdp(second, 1, fss)]
    corner = [hop_fsdp(by_x[0], 1, fss), hop_dp(by_y[1], 2, dps)]
    found = []
    for x, y, pair in ((0, 0, (first, second)), (1, 0, by_x), (0, 1, by_y), (1, 1, corner)):
        for base, part in ((0, pair[0]), (half, pair[1])):
            found.append((2 * x, 2 * base + y, part))
            found.append((2 * x + 1, 2 * base + y, hop_dp(part, 1, dps)))
    return found, along[-1]


def slots(found):
    return [
        (at, k, dp, fs + 2 * k)
        for at, (dp, fs, part) in enumerate(found)
        for k in range(part.shape[0])
    ]


def any_space():
    return pl.BlockSpec(memory_space=pl.ANY)


def in_vmem():
    return pl.BlockSpec(memory_space=pltpu.VMEM)


def lay_first_kernel(plan, count, ids_ref, *refs):
    parts, (w_ref, vec_ref, table_ref, bias_ref, stage, table_f32, sem) = refs[:count], refs[count:]
    copies = []
    for at, k, dp, fs in plan:
        copies.append(pltpu.make_async_copy(parts[at].at[k], stage.at[ids_ref[0] ^ dp, ids_ref[1] ^ fs], sem))
    for copy in copies:
        copy.start()
    for copy in copies:
        copy.wait()
    table_f32[...] = jnp.zeros_like(table_f32)
    for d in range(stage.shape[0]):
        for f in range(stage.shape[1]):
            rows, cols = stage.shape[2], 3 * D // stage.shape[1]
            w_ref[d * rows:(d + 1) * rows, f * cols:(f + 1) * cols] = stage[d, f, :, :cols]
            wide = D // stage.shape[1]
            small = stage[d, f, 0:16, cols:cols + wide].astype(F32)
            at = slice(f * wide, (f + 1) * wide)
            vec_ref[2 * d:2 * d + 2, at] = small[0:2]
            table_f32[5 * d:5 * d + 5, at] = small[2:7]
            bias_ref[0:1, d * D + f * wide:d * D + (f + 1) * wide] = small[7:8]
    table_ref[...] = table_f32[...].astype(BF16)


def lay_first(found, ids, sizes):
    parts = [part for _, _, part in found]
    rows, cols = parts[0].shape[1:]
    return pl.pallas_call(
        functools.partial(lay_first_kernel, slots(found), len(parts)),
        in_specs=[smem()] + [any_space()] * len(parts),
        out_specs=[in_vmem()] * 4,
        out_shape=[
            jax.ShapeDtypeStruct((D, 3 * D), BF16),
            jax.ShapeDtypeStruct((8, D), F32),
            jax.ShapeDtypeStruct((32, D), BF16),
            jax.ShapeDtypeStruct((1, FF), F32),
        ],
        scratch_shapes=[
            pltpu.VMEM(sizes + (rows, cols), BF16),
            pltpu.VMEM((32, D), F32),
            pltpu.SemaphoreType.DMA,
        ],
        compiler_params=params(),
        cost_estimate=pl.CostEstimate(flops=0, bytes_accessed=12_000_000, transcendentals=0),
        name="lay_first",
    )(ids, *parts)


def lay_up_kernel(plan, count, ids_ref, *refs):
    parts, (wu_ref, wo_ref, stage, sem) = refs[:count], refs[count:]
    dps, fss, rows, _ = stage.shape
    tall, wide = D // dps, FF // fss
    copies = []
    for at, k, dp, fs in plan:
        d, f = ids_ref[0] ^ dp, ids_ref[1] ^ fs
        rest = parts[at].at[k, pl.ds(tall, rows), :]
        copies.append(pltpu.make_async_copy(rest, stage.at[d, f], sem))
        there = wu_ref.at[pl.ds(pl.multiple_of(d * tall, tall), tall), pl.ds(pl.multiple_of(f * wide, wide), wide)]
        copies.append(pltpu.make_async_copy(parts[at].at[k, pl.ds(0, tall), :], there, sem))
    for copy in copies:
        copy.start()
    for copy in copies:
        copy.wait()
    narrow = D // fss
    for d in range(dps):
        for f in range(fss):
            for h in range(tall // rows):
                at = d * tall + h * rows
                wo_ref[at:at + rows, f * narrow:(f + 1) * narrow] = stage[d, f, :, h * narrow:(h + 1) * narrow]


def lay_up(found, ids, sizes):
    parts = [part for _, _, part in found]
    rows, cols = parts[0].shape[1:]
    return pl.pallas_call(
        functools.partial(lay_up_kernel, slots(found), len(parts)),
        in_specs=[smem()] + [any_space()] * len(parts),
        out_specs=[in_vmem()] * 2,
        out_shape=[jax.ShapeDtypeStruct((D, FF), BF16), jax.ShapeDtypeStruct((D, D), BF16)],
        scratch_shapes=[
            pltpu.VMEM(sizes + (rows - D // sizes[0], cols), BF16),
            pltpu.SemaphoreType.DMA,
        ],
        compiler_params=params(),
        cost_estimate=pl.CostEstimate(flops=0, bytes_accessed=12_000_000, transcendentals=0),
        name="lay_up",
    )(ids, *parts)


def lay_down_kernel(plan, count, ids_ref, *refs):
    parts, (wd_ref, sem) = refs[:count], refs[count:]
    tall, wide = parts[0].shape[1:]
    copies = []
    for at, k, dp, fs in plan:
        d, f = ids_ref[0] ^ dp, ids_ref[1] ^ fs
        there = wd_ref.at[pl.ds(pl.multiple_of(f * tall, tall), tall), pl.ds(pl.multiple_of(d * wide, wide), wide)]
        copies.append(pltpu.make_async_copy(parts[at].at[k], there, sem))
    for copy in copies:
        copy.start()
    for copy in copies:
        copy.wait()


def lay_down(found, ids):
    parts = [part for _, _, part in found]
    return pl.pallas_call(
        functools.partial(lay_down_kernel, slots(found), len(parts)),
        in_specs=[smem()] + [any_space()] * len(parts),
        out_specs=in_vmem(),
        out_shape=jax.ShapeDtypeStruct((D, FF), BF16),
        scratch_shapes=[pltpu.SemaphoreType.DMA],
        compiler_params=params(),
        cost_estimate=pl.CostEstimate(flops=0, bytes_accessed=10_000_000, transcendentals=0),
        name="lay_down",
    )(ids, *parts)


def order_rows(left_ref, plain, ordered, mine, count):
    plain[...] = left_ref[...].T
    tall = ordered.shape[0] // count
    for k in range(count):
        at = pl.multiple_of((mine ^ k) * tall, tall)
        ordered[k * tall:(k + 1) * tall, :] = plain[pl.ds(at, tall), :]


def cut_up_kernel(sizes, ids_ref, n2_ref, gh_ref, o_ref, gatt_ref, mine_ref, theirs_ref, plain, left, packed, full):
    dps, fss = sizes
    tall = D // dps
    step = pl.program_id(0)
    rows = mine_ref.shape[3] - tall
    narrow = D // fss

    @pl.when(step == 0)
    def _():
        order_rows(o_ref, plain, left, ids_ref[0], dps)
        full[...] = dot_nn(left[...], gatt_ref[...]).astype(BF16)
        for f in range(fss):
            for d in range(dps):
                for h in range(tall // rows):
                    at = d * tall + h * rows
                    packed[ids_ref[1] ^ f, d, :, h * narrow:(h + 1) * narrow] = full[at:at + rows, f * narrow:(f + 1) * narrow]
        order_rows(n2_ref, plain, left, ids_ref[0], dps)

    grad = dot_nn(left[...], gh_ref[...]).astype(BF16)
    for d in range(dps):
        ref = theirs_ref if d & 1 else mine_ref
        ref[d >> 1, 0, 0, :tall, :] = grad[d * tall:(d + 1) * tall]
        ref[d >> 1, 0, 0, tall:, :] = packed[step, d]


def cut_up(n2, gh, o, gatt, ids, sizes):
    dps, fss = sizes
    wide, tall = FF // fss, D // dps
    rows = tall * (D // fss) // wide
    shape = jax.ShapeDtypeStruct((dps // 2, 2, fss // 2, tall + rows, wide), BF16)
    block = pl.BlockSpec((dps // 2, 1, 1, tall + rows, wide), lambda i, ids: (0, i & 1, i >> 1, 0, 0))
    fixed = pl.BlockSpec((L, D), lambda i, ids: (0, 0))
    return pl.pallas_call(
        functools.partial(cut_up_kernel, sizes),
        grid_spec=pltpu.PrefetchScalarGridSpec(
            num_scalar_prefetch=1,
            grid=(fss,),
            in_specs=[fixed, pl.BlockSpec((L, wide), lambda i, ids: (0, i ^ ids[1])), fixed, fixed],
            out_specs=[block, block],
            scratch_shapes=[
                pltpu.VMEM((D, L), BF16),
                pltpu.VMEM((D, L), BF16),
                pltpu.VMEM((fss, dps, rows, wide), BF16),
                pltpu.VMEM((D, D), BF16),
            ],
        ),
        out_shape=[shape, shape],
        compiler_params=params(),
        cost_estimate=pl.CostEstimate(flops=2 * L * D * (FF + D), bytes_accessed=20_000_000, transcendentals=0),
        name="cut_up",
    )(ids, n2, gh, o, gatt)


def cut_down_kernel(sizes, ids_ref, gm_ref, a_ref, mine_ref, theirs_ref, plain, left):
    dps, fss = sizes
    step = pl.program_id(0)
    tall = D // fss

    @pl.when(step == 0)
    def _():
        order_rows(gm_ref, plain, left, ids_ref[1], fss)

    grad = dot_nn(left[...], a_ref[...]).astype(BF16)

    def store(ref):
        for f in range(fss):
            ref[0, f & 1, f >> 1] = grad[f * tall:(f + 1) * tall]

    @pl.when(step < dps // 2)
    def _():
        store(mine_ref)

    @pl.when(step >= dps // 2)
    def _():
        store(theirs_ref)


def cut_down(gm, a, ids, sizes):
    dps, fss = sizes
    half = dps // 2
    wide, tall = FF // dps, D // fss
    shape = jax.ShapeDtypeStruct((half, 2, fss // 2, tall, wide), BF16)
    block = (1, 2, fss // 2, tall, wide)

    def flip(i):
        return 2 * (i % half) + i // half

    return pl.pallas_call(
        functools.partial(cut_down_kernel, sizes),
        grid_spec=pltpu.PrefetchScalarGridSpec(
            num_scalar_prefetch=1,
            grid=(dps,),
            in_specs=[
                pl.BlockSpec((L, D), lambda i, ids: (0, 0)),
                pl.BlockSpec((L, wide), lambda i, ids: (0, flip(i) ^ ids[0])),
            ],
            out_specs=[
                pl.BlockSpec(block, lambda i, ids: (jnp.minimum(i, half - 1), 0, 0, 0, 0)),
                pl.BlockSpec(block, lambda i, ids: (jnp.maximum(i - half, 0), 0, 0, 0, 0)),
            ],
            scratch_shapes=[pltpu.VMEM((D, L), BF16), pltpu.VMEM((D, L), BF16)],
        ),
        out_shape=[shape, shape],
        compiler_params=params(),
        cost_estimate=pl.CostEstimate(flops=2 * L * D * FF, bytes_accessed=14_000_000, transcendentals=0),
        name="cut_down",
    )(ids, gm, a)


def cut_qkv_kernel(sizes, ids_ref, n1_ref, g_ref, small_ref, mine_ref, theirs_ref, plain, left, full):
    dps, fss = sizes
    tall, cols, wide = D // dps, 3 * D // fss, D // fss
    order_rows(n1_ref, plain, left, ids_ref[0], dps)
    for third in range(3):
        at = slice(third * D, (third + 1) * D)
        full[:, at] = dot_nn(left[...], g_ref[:, at]).astype(BF16)
    for f in range(fss):
        flip = ids_ref[1] ^ f
        for d in range(dps):
            ref = theirs_ref if d & 1 else mine_ref
            rows = slice(d * tall, (d + 1) * tall)
            ref[d >> 1, flip & 1, flip >> 1, :, :cols] = full[rows, f * cols:(f + 1) * cols]
            own = small_ref[ids_ref[0] ^ d, :, f * wide:(f + 1) * wide].astype(BF16)
            ref[d >> 1, flip & 1, flip >> 1, :, cols:] = jnp.zeros((tall, wide), BF16)
            ref[d >> 1, flip & 1, flip >> 1, 0:16, cols:] = own


def cut_qkv(n1, gqkv, small, ids, sizes):
    dps, fss = sizes
    shape = jax.ShapeDtypeStruct((dps // 2, 2, fss // 2, D // dps, 4 * D // fss), BF16)
    return pl.pallas_call(
        functools.partial(cut_qkv_kernel, sizes),
        in_specs=[smem()] + [in_vmem()] * 3,
        out_specs=[in_vmem()] * 2,
        out_shape=[shape, shape],
        scratch_shapes=[pltpu.VMEM((D, L), BF16), pltpu.VMEM((D, L), BF16), pltpu.VMEM((D, 3 * D), BF16)],
        compiler_params=params(),
        cost_estimate=pl.CostEstimate(flops=2 * L * D * 3 * D, bytes_accessed=12_000_000, transcendentals=0),
        name="cut_qkv",
    )(ids, n1, gqkv, small)


def plus(*terms):
    return sum(term.astype(F32) for term in terms)


def reduce_shards(mine, theirs, sizes):
    dps, fss = sizes
    deep = fss // 2
    half = deep // 2
    both = plus(mine, hop_dp(theirs, 1, dps)).astype(BF16)
    first, second = both[:, :, :half], both[:, :, half:]
    got_x = hop_dp(first[1], 2, dps)
    got_y = hop_fsdp(second[:, 1], 1, fss)
    first = plus(first[0], got_x).astype(BF16)
    second = plus(second[:, 0], got_y).astype(BF16)
    got_y = hop_fsdp(first[1], 1, fss)
    got_x = hop_dp(second[1], 2, dps)
    first = plus(first[0], got_y).astype(BF16)
    second = plus(second[0], got_x).astype(BF16)
    apart = [first[k] for k in range(half)] + [second[k] for k in range(deep - half)]
    return plus(apart[0], *[hop_fsdp(apart[z], 2 * z, fss) for z in range(1, deep)])


def compute(tokens, lengths, lead_index, cotangent, weights, reduce_down, reduce_up, reduce_qkv):
    w_qkv, vec, table, bias, w_up, w_out, w_down_t = weights
    x, gy = tokens.reshape(L, D), cotangent.reshape(L, D)
    n1, qkv = qkv_call(lengths, lead_index, x, vec, table, w_qkv)
    o, lse = attend_call(lengths, qkv)
    middle, n2, a, slope = up_call(o, x, vec, w_out, w_up, bias)
    down = reduce_down(gy, a)
    gh, gmid, gatt, go, sums, bup = feed_back_call(gy, slope, middle, vec, w_down_t, w_up, w_out)
    up, out = reduce_up(n2, gh, o, gatt)
    gqkv, qsums = attend_back_call(lengths, qkv, o, go, lse)
    gx, first_sums, gtable = first_back_call(lengths, lead_index, x, gmid, gqkv, vec, w_qkv)
    gvec = jnp.concatenate([first_sums[:2], sums[:2], qsums[:2], sums[2:4]], axis=0)
    qkv_grad, gvec, gtable, gbias = reduce_qkv(n1, gqkv, gvec, gtable[:LEADS], bup[0].reshape(FF // D, D))
    y = down_call(a, middle, vec, w_down_t)
    return y.reshape(1, L, D), gx.reshape(1, L, D), qkv_grad, out, up, down, gvec, gtable, gbias


def per_device(sizes, tokens, lengths, lead_index, cotangent, w_qkv, w_out, w_up, w_down, vectors, table, bias):
    dps, fss = sizes
    ids = jnp.stack([lax.axis_index("dp"), lax.axis_index("fsdp")]).astype(jnp.int32)
    narrow, wide, tall = D // fss, FF // fss, D // dps
    fold = wide // narrow
    small = jnp.concatenate([vectors, table, bias], axis=0)
    piece = jnp.concatenate([w_qkv, jnp.pad(small, ((0, tall - small.shape[0]), (0, 0)))], axis=1)
    found, done = gather_shards(piece, sizes)
    w_qkv, vec, table, bias = lay_first(found, ids, sizes)
    rows = tall // fold
    folded = jnp.concatenate([w_out[k * rows:(k + 1) * rows] for k in range(fold)], axis=1)
    piece = after(jnp.concatenate([w_up, folded], axis=0), done)
    found, done = gather_shards(piece, sizes)
    w_up, w_out = lay_up(found, ids, sizes)
    piece = after(w_down.T, done)
    found, done = gather_shards(piece, sizes)
    w_down_t = lay_down(found, ids)

    def reduce_down(gm, a):
        return reduce_shards(*cut_down(gm, a, ids, sizes), sizes).T

    def reduce_up(n2, gh, o, gatt):
        got = reduce_shards(*cut_up(n2, gh, o, gatt, ids, sizes), sizes)
        out = jnp.concatenate([got[tall:, k * narrow:(k + 1) * narrow] for k in range(fold)], axis=0)
        return got[:tall], out

    def reduce_qkv(n1, gqkv, gvec, gtable, gbias):
        parts = [gvec.reshape(dps, -1, D), gtable.reshape(dps, -1, D), gbias.reshape(dps, -1, D)]
        parts = jnp.concatenate(parts, axis=1)
        parts = jnp.pad(parts, ((0, 0), (0, 16 - parts.shape[1]), (0, 0)))
        got = reduce_shards(*cut_qkv(n1, gqkv, parts, ids, sizes), sizes)
        cols = 3 * narrow
        return got[:, :cols], got[0:2, cols:], got[2:7, cols:], got[7:8, cols:]

    weights = (w_qkv, vec, table, bias, w_up, w_out, w_down_t)
    return compute(tokens, lengths, lead_index, cotangent, weights, reduce_down, reduce_up, reduce_qkv)


def per_device_plain(sizes, tokens, lengths, lead_index, cotangent, w_qkv, w_out, w_up, w_down, vectors, table, bias):
    def full(shard):
        return lax.all_gather(lax.all_gather(shard, "fsdp", axis=1, tiled=True), "dp", axis=0, tiled=True)

    def share(grad):
        part = lax.psum_scatter(grad.astype(F32), "fsdp", scatter_dimension=1, tiled=True)
        return lax.psum_scatter(part, "dp", scatter_dimension=0, tiled=True)

    weights = (
        full(w_qkv),
        full(vectors).astype(F32),
        jnp.pad(full(table), ((0, 32 - LEADS), (0, 0))),
        full(bias).astype(F32).reshape(1, FF),
        full(w_up),
        full(w_out),
        full(w_down).T,
    )

    def reduce_down(gm, a):
        return share(outer_call(gm, a, "grad_down").T)

    def reduce_up(n2, gh, o, gatt):
        return share(outer_call(n2, gh, "grad_up")), share(outer_call(o, gatt, "grad_out"))

    def reduce_qkv(n1, gqkv, gvec, gtable, gbias):
        return share(outer_call(n1, gqkv, "grad_qkv")), share(gvec), share(gtable), share(gbias)

    return compute(tokens, lengths, lead_index, cotangent, weights, reduce_down, reduce_up, reduce_qkv)


def solution(mesh):
    sizes = (mesh.shape["dp"], mesh.shape["fsdp"])
    lanes = FF // sizes[1]
    plan = per_device if lanes % 128 == 0 and sizes[0] == 4 and sizes[1] % 4 == 0 else per_device_plain
    rows, both = P(("dp", "fsdp"), None, None), P("dp", "fsdp")
    index = P(("dp", "fsdp"), None)
    return jax.shard_map(
        functools.partial(plan, sizes),
        mesh=mesh,
        in_specs=(rows, index, index, rows) + (both,) * 7,
        out_specs=(rows, rows) + (both,) * 7,
        check_vma=False,
    )
```

time: 1350 us -> 401 us (0.30)
  waiting for transfers between devices: 664 us -> 115 us
  matrix products: 303 us -> 0 us
  Pallas kernels: 0 us -> 192 us
  blocking collectives: 131 us -> 0 us
  local copies, waits for them, and re-layouts: 121 us -> 10.4 us
  other arithmetic: 94.8 us -> 12.2 us
  starting transfers between devices: 0.62 us -> 63.7 us
  between operations: 16.2 us -> 1.96 us
    reduce_scatter x6 -> x0, waiting for transfers between devices: 449 us -> none  [the longest x1 162 us: per_device(): lax.psum_scatter(grad_down, 'fsdp', scatter_dimension=1, tiled=True)]
    dot_general x27 -> x0, matrix products: 297 us -> none  [the longest x4 46.9 us: masked_scores(): jnp.einsum('qhd,khd->hqk', query_block, key_heads, preferred_element_type...]
    unnamed x20 -> x0, waiting for transfers between devices: 215 us -> none
    pallas_call x0 -> x13, Pallas kernels: none -> 192 us  [the longest x1 44.7 us: attend_back_call(): pl.pallas_call(attend_back_kernel, in_specs=[smem()] + [pl.BlockSpec(memo...]
    all_gather x10 -> x0, blocking collectives: 126 us -> none  [the longest x1 31 us: collect(): lax.all_gather(across[5], 'fsdp', axis=1, tiled=True)]
    ppermute x0 -> x75, waiting for transfers between devices: none -> 115 us  [the longest x33 69 us: hop_fsdp(): return lax.ppermute(value, 'fsdp', [(i, i ^ flip) for i in range(ranks)])]
    ppermute x0 -> x75, starting transfers between devices: none -> 63.7 us  [the longest x33 38.4 us: hop_fsdp(): return lax.ppermute(value, 'fsdp', [(i, i ^ flip) for i in range(ranks)])]
    dynamic_update_slice x4 -> x0, local copies, waits for them, and re-layouts: 56.7 us -> none  [attend_row(): mixture, log_total = lax.map(attend_block, (query_blocks, window_blocks))]
  transfers between devices with their start and end apart: 15 -> 75, of which waited for: 10 -> 28; matrix products, arithmetic and copies ran while one was open for 34% -> 3% of each run, Pallas kernels for 0% -> 20%
where the time goes in v1:
time: 401 us; the launch traced here: 396 us
  Pallas kernels  192 us (48%)
  waiting for transfers between devices  115 us (29%)
  starting transfers between devices  63.7 us (16%)
  other arithmetic  12.2 us (3%)
  local copies, waits for them, and re-layouts  10.4 us (3%)
    ppermute x33, waiting for transfers between devices, hop_fsdp(): return lax.ppermute(value, 'fsdp', [(i, i ^ flip) for i in range(ranks)])  69 us
    ppermute x42, waiting for transfers between devices, hop_dp(): return lax.ppermute(value, 'dp', [(i, i ^ flip) for i in range(ranks)])  46.1 us
    pallas_call x1, Pallas kernels, attend_back_call(): pl.pallas_call(attend_back_kernel, in_specs=[smem()] + [pl.BlockSpec(memo...  44.7 us
    ppermute x33, starting transfers between devices, hop_fsdp(): return lax.ppermute(value, 'fsdp', [(i, i ^ flip) for i in range(ranks)])  38.4 us
    ppermute x42, starting transfers between devices, hop_dp(): return lax.ppermute(value, 'dp', [(i, i ^ flip) for i in range(ranks)])  25.3 us
    pallas_call x1, Pallas kernels, up_call(): pl.pallas_call(up_kernel, grid=(TILES,), in_specs=[rows_of(D), rows_of(D)...  23 us
    pallas_call x1, Pallas kernels, feed_back_call(): pl.pallas_call(feed_back_kernel, grid=(TILES,), in_specs=[rows_of(D), row...  20.5 us
    pallas_call x1, Pallas kernels, attend_call(): pl.pallas_call(attend_kernel, in_specs=[smem(), pl.BlockSpec(memory_space...  19 us
  transfers between devices with their start and end apart: 75, of which 28 were waited for; matrix products, arithmetic and copies ran while one was open for 3% of the time, Pallas kernels for 20%

profile of v1, /device:TPU:0, one launch (start us, length us, event | category | flops | bytes accessed | tf_op | source)
XLA Modules:
  0.0 395.5 jit_solution(7567518438098819153)
XLA Ops:
  2.4 4.1 %collective-permute-start.2 = (bf16[192,384]{1,0:T(8,128)(2,1)S(1)}, bf16[192,384]{1,0:T(8,128)(2,1)S(1)}, u32[]{:S(2)}, u32[]{:S(2)}) collective-permute-start(bf16[192,384]{1,0:T(8,128)(2,1)S(1)} %pad_maximum_fusion.6), channel_id=1, source_target_pairs={{0,4},{1,5},{2,6},{3,7},{4,0},{5,1},{6,2},{7,3},{8,12},{9,13},{10,... | collective-permute-start | bytes 442376 | tf_op jit(solution)/shard_map/ppermute | solution.py:470
  6.5 1.6 collective-permute-start
  9.8 8.0 %collective-permute-done.3 = bf16[192,384]{1,0:T(8,128)(2,1)S(1)} collective-permute-done((bf16[192,384]{1,0:T(8,128)(2,1)S(1)}, bf16[192,384]{1,0:T(8,128)(2,1)S(1)}, u32[]{:S(2)}, u32[]{:S(2)}) %collective-permute-start.3) | collective-permute-done | bytes 147488 | tf_op jit(solution)/shard_map/ppermute | solution.py:470
  17.9 2.5 collective-permute-start.20
  20.3 2.1 collective-permute-start.19
  23.1 1.6 collective-permute-start.11
  25.7 1.6 collective-permute-start.7
  27.3 9.8 %collective-permute-done.19 = bf16[240,384]{1,0:T(8,128)(2,1)S(1)} collective-permute-done((bf16[240,384]{1,0:T(8,128)(2,1)S(1)}, bf16[240,384]{1,0:T(8,128)(2,1)S(1)}, u32[]{:S(2)}, u32[]{:S(2)}) %collective-permute-start.19) | collective-permute-done | bytes 184352 | tf_op jit(solution)/shard_map/ppermute | solution.py:470
  37.1 1.5 collective-permute-start.9
  38.6 1.5 collective-permute-start.5
  40.8 2.5 collective-permute-start.37
  43.3 3.6 collective-permute-done.9.refs_8_
  47.3 2.7 collective-permute-start.34
  50.1 1.6 collective-permute-start.22
  51.6 3.8 collective-permute-done.36
  55.5 1.5 collective-permute-start.28
  58.3 2.1 collective-permute-start.15
  60.4 5.0 %collective-permute-done.28.refs_10_ = bf16[2,240,384]{2,1,0:T(8,128)(2,1)S(1)} collective-permute-done((bf16[2,240,384]{2,1,0:T(8,128)(2,1)S(1)}, bf16[2,240,384]{2,1,0:T(8,128)(2,1)S(1)}, u32[]{:S(2)}, u32[]{:S(2)}) %collective-permute-start.28) | collective-permute-done | bytes 368672 | tf_op jit(solution)/shard_map/ppermute | solution.py:470
  65.4 3.2 collective-permute-done.24.refs_6_
  69.5 3.5 collective-permute-done.15.refs_14_
  73.0 1.1 collective-permute-start.43
  74.1 1.5 collective-permute-start.39
  75.7 2.7 collective-permute-done.13.refs_12_
  79.0 1.7 collective-permute-start.41
  80.7 4.1 %collective-permute-done.43.refs_8_ = bf16[2,96,768]{2,1,0:T(8,128)(2,1)S(1)} collective-permute-done((bf16[2,96,768]{2,1,0:T(8,128)(2,1)S(1)}, bf16[2,96,768]{2,1,0:T(8,128)(2,1)S(1)}, u32[]{:S(2)}, u32[]{:S(2)}) %collective-permute-start.43) | collective-permute-done | bytes 294944 | tf_op jit(solution)/shard_map/ppermute | solution.py:470
  85.4 5.3 %collective-permute-done.45.refs_10_ = bf16[2,96,768]{2,1,0:T(8,128)(2,1)S(1)} collective-permute-done((bf16[2,96,768]{2,1,0:T(8,128)(2,1)S(1)}, bf16[2,96,768]{2,1,0:T(8,128)(2,1)S(1)}, u32[]{:S(2)}, u32[]{:S(2)}) %collective-permute-start.45) | collective-permute-done | bytes 294944 | tf_op jit(solution)/shard_map/ppermute | solution.py:470
  91.4 1.7 collective-permute-start.49
  93.9 6.3 %collective-permute-done.47.refs_12_ = bf16[2,96,768]{2,1,0:T(8,128)(2,1)} collective-permute-done((bf16[2,96,768]{2,1,0:T(8,128)(2,1)S(1)}, bf16[2,96,768]{2,1,0:T(8,128)(2,1)}, u32[]{:S(2)}, u32[]{:S(2)}) %collective-permute-start.47) | collective-permute-done | bytes 294944 | tf_op jit(solution)/shard_map/ppermute | solution.py:470
  100.8 1.8 collective-permute-start.32
  104.0 6.4 %lay_first.1 = (bf16[768,2304]{1,0:T(8,128)(2,1)}, f32[8,768]{1,0:T(8,128)}, bf16[32,768]{1,0:T(8,128)(2,1)}, f32[1,3072]{1,0:T(1,128)}) custom-call(s32[2]{0:T(128)} %pad_add_fusion.ids_ref, bf16[2,192,384]{2,1,0:T(8,128)(2,1)} %copy-done.6, bf16[2,192,384]{2,1,0:T(8,128)(2,1)} %copy-done.27, bf16[2,192,384]{2,1,0:T(8,128)(2,1)} %copy-done.5, ...), custom_call_target="tpu_custom_call" | custom-call | bytes 12000000 | tf_op jit(solution)/shard_map/lay_first/pallas_call | solution.py:536
  112.4 9.3 %norm_qkv.1 = (bf16[1024,768]{1,0:T(8,128)(2,1)}, bf16[1024,2304]{1,0:T(8,128)(2,1)}) custom-call(s32[1,8]{1,0:T(1,128)} %len_ref.7, s32[1,8]{1,0:T(1,128)} %lead_ref.3, bf16[1024,768]{1,0:T(8,128)(2,1)} %bitcast.163, f32[8,768]{1,0:T(8,128)} %get-tuple-element.42.vec_ref, bf16[32,768]{1,0:T(8,128)(2,1)} %get-tuple-element.43.table_ref, ...), custom_call_target="tpu_custom_call" | custom-call | flops 3623878656 | bytes 12000000 | tf_op jit(solution)/shard_map/norm_qkv/pallas_call | solution.py:97
  121.7 19.0 %attend.1 = (bf16[1024,768]{1,0:T(8,128)(2,1)}, f32[16,1024]{1,0:T(8,128)}) custom-call(s32[1,8]{1,0:T(1,128)} %len_ref.7, bf16[1024,2304]{1,0:T(8,128)(2,1)} %get-tuple-element.45.qkv_ref), custom_call_target="tpu_custom_call" | custom-call | flops 3221225472 | bytes 8000000 | tf_op jit(solution)/shard_map/attend/pallas_call | solution.py:190
  140.7 5.3 %lay_down.1.wdt_ref = bf16[768,3072]{1,0:T(8,128)(2,1)} custom-call(s32[2]{0:T(128)} %pad_add_fusion.ids_ref, bf16[2,96,768]{2,1,0:T(8,128)(2,1)} %copy-done.7, bf16[2,96,768]{2,1,0:T(8,128)(2,1)} %copy-done.31, bf16[2,96,768]{2,1,0:T(8,128)(2,1)} %copy-done.8, bf16[2,96,768]{2,1,0:T(8,128)(2,1)} %copy-done.36, bf16[2,96,768]{2,1,0:T(8,128)(2,1)} %copy-done.29, ...), custom_call_target="tpu_custom_call" | custom-call | bytes 10000000 | tf_op jit(solution)/shard_map/lay_down/pallas_call | solution.py:614
  147.9 6.0 %lay_up.1 = (bf16[768,3072]{1,0:T(8,128)(2,1)}, bf16[768,768]{1,0:T(8,128)(2,1)}) custom-call(s32[2]{0:T(128)} %pad_add_fusion.ids_ref, bf16[2,240,384]{2,1,0:T(8,128)(2,1)} %copy-done.3, bf16[2,240,384]{2,1,0:T(8,128)(2,1)} %copy-done.11, bf16[2,240,384]{2,1,0:T(8,128)(2,1)} %copy-done.4, bf16[2,240,384]{2,1,0:T(8,128)(2,1)} %copy-done.15, ...), custom_call_target="tpu_custom_call" | custom-call | bytes 12000000 | tf_op jit(solution)/shard_map/lay_up/pallas_call | solution.py:583
  153.9 23.0 %feed_up.1 = (f32[1024,768]{1,0:T(8,128)}, bf16[1024,768]{1,0:T(8,128)(2,1)}, bf16[1024,3072]{1,0:T(8,128)(2,1)}, bf16[1024,3072]{1,0:T(8,128)(2,1)}) custom-call(bf16[1024,768]{1,0:T(8,128)(2,1)} %get-tuple-element.46.o_ref, bf16[1024,768]{1,0:T(8,128)(2,1)} %bitcast.164, f32[8,768]{1,0:T(8,128)} %get-tuple-element.42.vec_ref, ...), custom_call_target="tpu_custom_call" | custom-call | flops 6039797760 | bytes 25000000 | tf_op jit(solution)/shard_map/feed_up/pallas_call | solution.py:311
  176.9 20.5 %feed_back.1 = (bf16[1024,3072]{1,0:T(8,128)(2,1)}, f32[1024,768]{1,0:T(8,128)}, bf16[1024,768]{1,0:T(8,128)(2,1)}, bf16[1024,768]{1,0:T(8,128)(2,1)}, f32[8,768]{1,0:T(8,128)}, /*index=5*/f32[8,3072]{1,0:T(8,128)}) custom-call(bf16[1024,768]{1,0:T(8,128)(2,1)} %bitcast.166, bf16[1024,3072]{1,0:T(8,128)(2,1)} %get-tuple-element.54.slope_ref, ...), custom_call_target="tpu_custom_call" | custom-call | flops 10871635968 | bytes 35000000 | tf_op jit(solution)/shard_map/feed_back/pallas_call | solution.py:383
  197.4 44.7 %attend_back.1 = (bf16[1024,2304]{1,0:T(8,128)(2,1)}, f32[8,768]{1,0:T(8,128)}) custom-call(s32[1,8]{1,0:T(1,128)} %len_ref.7, bf16[1024,2304]{1,0:T(8,128)(2,1)} %get-tuple-element.45.qkv_ref, bf16[1024,768]{1,0:T(8,128)(2,1)} %get-tuple-element.46.o_ref, bf16[1024,768]{1,0:T(8,128)(2,1)} %get-tuple-element.56.go_ref, f32[16,1024]{1,0:T(8,128)} %get-tuple-element.57.lse_ref), custom_call_target="tpu_custom_call" | custom-call | flops 8053063680 | bytes 15000000 | tf_op jit(solution)/shard_map/attend_back/pallas_call | solution.py:265
  242.9 10.4 %first_back.1 = (f32[1024,768]{1,0:T(8,128)}, f32[8,768]{1,0:T(8,128)}, f32[32,768]{1,0:T(8,128)}) custom-call(s32[1,8]{1,0:T(1,128)} %len_ref.7, s32[1,8]{1,0:T(1,128)} %lead_ref.3, bf16[1024,768]{1,0:T(8,128)(2,1)} %bitcast.165, f32[1024,768]{1,0:T(8,128)} %get-tuple-element.55.gmid_ref, bf16[1024,2304]{1,0:T(8,128)(2,1)} %get-tuple-element.58.g_ref, ...), custom_call_target="tpu_custom_call" | custom-call | flops 3623878656 | bytes 17000000 | tf_op jit(solution)/shard_map/first_back/pallas_call | solution.py:449
  256.6 10.0 %cut_qkv.1 = (bf16[2,2,4,192,384]{4,3,2,1,0:T(8,128)(2,1)}, bf16[2,2,4,192,384]{4,3,2,1,0:T(8,128)(2,1)}) custom-call(s32[2]{0:T(128)} %pad_add_fusion.ids_ref, bf16[1024,768]{1,0:T(8,128)(2,1)} %get-tuple-element.60.n1_ref, bf16[1024,2304]{1,0:T(8,128)(2,1)} %get-tuple-element.58.g_ref, f32[4,16,768]{2,1,0:T(8,128)} %select_maximum_fusion.small_ref), custom_call_target="tpu_custom_call" | custom-call | flops 3623878656 | bytes 12000000 | tf_op jit(solution)/shard_map/cut_qkv/pallas_call | solution.py:764
  266.9 11.1 %cut_down.1 = (bf16[2,2,4,96,768]{4,3,2,1,0:T(8,128)(2,1)}, bf16[2,2,4,96,768]{4,3,2,1,0:T(8,128)(2,1)}) custom-call(s32[2]{0:T(128)} %pad_add_fusion.ids_ref, bf16[1024,768]{1,0:T(8,128)(2,1)} %bitcast.167, bf16[1024,3072]{1,0:T(8,128)(2,1)} %get-tuple-element.51.a_ref), custom_call_target="tpu_custom_call" | custom-call | flops 4831838208 | bytes 14000000 | tf_op jit(solution)/shard_map/cut_down/pallas_call | solution.py:721
  278.2 16.2 %cut_up.1 = (bf16[2,2,4,240,384]{4,3,2,1,0:T(8,128)(2,1)}, bf16[2,2,4,240,384]{4,3,2,1,0:T(8,128)(2,1)}) custom-call(s32[2]{0:T(128)} %pad_add_fusion.ids_ref, bf16[1024,768]{1,0:T(8,128)(2,1)} %get-tuple-element.68.n2_ref, bf16[1024,3072]{1,0:T(8,128)(2,1)} %get-tuple-element.69.gh_ref, bf16[1024,768]{1,0:T(8,128)(2,1)} %get-tuple-element.46.o_ref, ...), custom_call_target="tpu_custom_call" | custom-call | flops 6039797760 | bytes 20000000 | tf_op jit(solution)/shard_map/cut_up/pallas_call | solution.py:666
  294.7 10.3 %feed_down.1 = bf16[1024,768]{1,0:T(8,128)(2,1)} custom-call(bf16[1024,3072]{1,0:T(8,128)(2,1)} %get-tuple-element.51.a_ref, f32[1024,768]{1,0:T(8,128)} %get-tuple-element.52.mid_ref, f32[8,768]{1,0:T(8,128)} %get-tuple-element.42.vec_ref, bf16[768,3072]{1,0:T(8,128)(2,1)} %lay_down.1.wdt_ref), custom_call_target="tpu_custom_call" | custom-call | flops 4831838208 | bytes 17000000 | tf_op jit(solution)/shard_map/feed_down/pallas_call | solution.py:333
  305.0 2.3 add_convert_fusion.2
  307.5 1.7 collective-permute-start.52
  310.0 1.4 collective-permute-start.68
  311.5 1.1 collective-permute-start.71
  312.6 11.1 %collective-permute-done.52 = bf16[2,2,192,384]{3,2,1,0:T(8,128)(2,1)S(1)} collective-permute-done((bf16[2,2,192,384]{3,2,1,0:T(8,128)(2,1)S(1)}, bf16[2,2,192,384]{3,2,1,0:T(8,128)(2,1)S(1)}, u32[]{:S(2)}, u32[]{:S(2)}) %collective-permute-start.52) | collective-permute-done | bytes 589856 | tf_op jit(solution)/shard_map/ppermute | solution.py:466
  323.7 1.8 collective-permute-done.55
  326.4 9.9 %collective-permute-done.68 = bf16[2,2,96,768]{3,2,1,0:T(8,128)(2,1)S(1)} collective-permute-done((bf16[2,2,96,768]{3,2,1,0:T(8,128)(2,1)S(1)}, bf16[2,2,96,768]{3,2,1,0:T(8,128)(2,1)S(1)}, u32[]{:S(2)}, u32[]{:S(2)}) %collective-permute-start.68) | collective-permute-done | bytes 589856 | tf_op jit(solution)/shard_map/ppermute | solution.py:466
  336.3 1.8 collective-permute-done.71
  339.9 1.7 collective-permute-start.60
  342.6 1.1 collective-permute-start.63
  344.4 1.2 collective-permute-start.57
  345.7 5.0 %collective-permute-done.69 = bf16[2,96,768]{2,1,0:T(8,128)(2,1)S(1)} collective-permute-done((bf16[2,96,768]{2,1,0:T(8,128)(2,1)S(1)}, bf16[2,96,768]{2,1,0:T(8,128)(2,1)S(1)}, u32[]{:S(2)}, u32[]{:S(2)}) %collective-permute-start.69) | collective-permute-done | bytes 294944 | tf_op jit(solution)/shard_map/ppermute | solution.py:470
  351.5 1.2 collective-permute-start.54
  352.8 11.3 %collective-permute-done.60 = bf16[2,2,240,384]{3,2,1,0:T(8,128)(2,1)S(1)} collective-permute-done((bf16[2,2,240,384]{3,2,1,0:T(8,128)(2,1)S(1)}, bf16[2,2,240,384]{3,2,1,0:T(8,128)(2,1)S(1)}, u32[]{:S(2)}, u32[]{:S(2)}) %collective-permute-start.60) | collective-permute-done | bytes 737312 | tf_op jit(solution)/shard_map/ppermute | solution.py:466
  365.4 1.6 collective-permute-start.74
  368.1 1.5 collective-permute-start.64
  372.0 5.2 %collective-permute-done.64 = bf16[2,240,384]{2,1,0:T(8,128)(2,1)S(1)} collective-permute-done((bf16[2,240,384]{2,1,0:T(8,128)(2,1)S(1)}, bf16[2,240,384]{2,1,0:T(8,128)(2,1)S(1)}, u32[]{:S(2)}, u32[]{:S(2)}) %collective-permute-start.64) | collective-permute-done | bytes 368672 | tf_op jit(solution)/shard_map/ppermute | solution.py:466
  377.3 2.1 collective-permute-start.65
  379.5 1.1 collective-permute-done.61
  380.5 1.7 collective-permute-start.66
  384.1 7.8 %collective-permute-done.65 = bf16[240,384]{1,0:T(8,128)(2,1)S(1)} collective-permute-done((bf16[240,384]{1,0:T(8,128)(2,1)S(1)}, bf16[240,384]{1,0:T(8,128)(2,1)S(1)}, u32[]{:S(2)}, u32[]{:S(2)}) %collective-permute-start.65) | collective-permute-done | bytes 184352 | tf_op jit(solution)/shard_map/ppermute | solution.py:470
  391.8 1.7 collective-permute-done.62
  (251 shorter events, 36.0 us)
Async XLA Ops:
  2.4 20.6 %collective-permute-start.2 = (bf16[192,384]{1,0:T(8,128)(2,1)S(1)}, bf16[192,384]{1,0:T(8,128)(2,1)S(1)}, u32[]{:S(2)}, u32[]{:S(2)}) collective-permute-start(bf16[192,384]{1,0:T(8,128)(2,1)S(1)} %pad_maximum_fusion.6), channel_id=1, source_target_pairs={{0,4},{1,5},{2,6},{3,7},{4,0},{5,1},{6,2},{7,3},{8,12},{9,13},{10,... | collective-permute-start | bytes 442376 | tf_op jit(solution)/shard_map/ppermute | solution.py:470
  6.5 19.2 %collective-permute-start = (bf16[192,384]{1,0:T(8,128)(2,1)S(1)}, bf16[192,384]{1,0:T(8,128)(2,1)S(1)}, u32[]{:S(2)}, u32[]{:S(2)}) collective-permute-start(bf16[192,384]{1,0:T(8,128)(2,1)S(1)} %pad_maximum_fusion.6), channel_id=1, source_target_pairs={{0,2},{1,3},{2,0},{3,1},{4,6},{5,7},{6,4},{7,5},{8,10},{9,11},{10,... | collective-permute-start | bytes 442376 | tf_op jit(solution)/shard_map/ppermute | solution.py:470
  8.1 9.8 %collective-permute-start.3 = (bf16[192,384]{1,0:T(8,128)(2,1)S(1)}, bf16[192,384]{1,0:T(8,128)(2,1)S(1)}, u32[]{:S(2)}, u32[]{:S(2)}) collective-permute-start(bf16[192,384]{1,0:T(8,128)(2,1)S(1)} %pad_maximum_fusion.6), channel_id=1, source_target_pairs={{0,6},{1,7},{2,4},{3,5},{4,2},{5,3},{6,0},{7,1},{8,14},{9,15},{10,... | collective-permute-start | bytes 442376 | tf_op jit(solution)/shard_map/ppermute | solution.py:470
  17.9 9.4 %collective-permute-start.20 = (bf16[240,384]{1,0:T(8,128)(2,1)S(1)}, bf16[240,384]{1,0:T(8,128)(2,1)S(1)}, u32[]{:S(2)}, u32[]{:S(2)}) collective-permute-start(bf16[240,384]{1,0:T(8,128)(2,1)S(1)} %maximum_maximum_fusion), channel_id=1, source_target_pairs={{0,6},{1,7},{2,4},{3,5},{4,2},{5,3},{6,0},{7,1},{8,14},{9,15},{10,... | collective-permute-start | bytes 552968 | tf_op jit(solution)/shard_map/ppermute | solution.py:470
  20.3 16.7 %collective-permute-start.19 = (bf16[240,384]{1,0:T(8,128)(2,1)S(1)}, bf16[240,384]{1,0:T(8,128)(2,1)S(1)}, u32[]{:S(2)}, u32[]{:S(2)}) collective-permute-start(bf16[240,384]{1,0:T(8,128)(2,1)S(1)} %maximum_maximum_fusion), channel_id=1, source_target_pairs={{0,4},{1,5},{2,6},{3,7},{4,0},{5,1},{6,2},{7,3},{8,12},{9,13},{10,... | collective-permute-start | bytes 552968 | tf_op jit(solution)/shard_map/ppermute | solution.py:470
  22.5 16.1 %collective-permute-start.17 = (bf16[240,384]{1,0:T(8,128)(2,1)S(1)}, bf16[240,384]{1,0:T(8,128)(2,1)S(1)}, u32[]{:S(2)}, u32[]{:S(2)}) collective-permute-start(bf16[240,384]{1,0:T(8,128)(2,1)S(1)} %maximum_maximum_fusion), channel_id=1, source_target_pairs={{0,2},{1,3},{2,0},{3,1},{4,6},{5,7},{6,4},{7,5},{8,10},{9,11},{10,... | collective-permute-start | bytes 552968 | tf_op jit(solution)/shard_map/ppermute | solution.py:470
  23.1 17.0 %collective-permute-start.11 = (bf16[2,192,384]{2,1,0:T(8,128)(2,1)S(1)}, bf16[2,192,384]{2,1,0:T(8,128)(2,1)S(1)}, u32[]{:S(2)}, u32[]{:S(2)}) collective-permute-start(bf16[2,192,384]{2,1,0:T(8,128)(2,1)S(1)} %pad_maximum_fusion.3.refs_2_), channel_id=1, source_target_pairs={{0,1},{1,0},{2,3},{3,2},{4,5},{5,4},{6,7},{7,6},{8,9},{9,8},{10,11... | collective-permute-start | bytes 884744 | tf_op jit(solution)/shard_map/ppermute | solution.py:470
  25.7 14.5 %collective-permute-start.7 = (bf16[2,192,384]{2,1,0:T(8,128)(2,1)S(1)}, bf16[2,192,384]{2,1,0:T(8,128)(2,1)S(1)}, u32[]{:S(2)}, u32[]{:S(2)}) collective-permute-start(bf16[2,192,384]{2,1,0:T(8,128)(2,1)S(1)} %pad_maximum_fusion.3.refs_2_), channel_id=1, source_target_pairs={{0,16},{8,24},{16,0},{24,8},{1,17},{9,25},{17,1},{25,9},{2,18},{10... | collective-permute-start | bytes 884744 | tf_op jit(solution)/shard_map/ppermute | solution.py:466
  27.2 13.5 %collective-permute-start.4 = (bf16[2,192,384]{2,1,0:T(8,128)(2,1)S(1)}, bf16[2,192,384]{2,1,0:T(8,128)(2,1)S(1)}, u32[]{:S(2)}, u32[]{:S(2)}) collective-permute-start(bf16[2,192,384]{2,1,0:T(8,128)(2,1)S(1)} %pad_maximum_fusion.3.refs_2_), channel_id=1, source_target_pairs={{0,8},{8,0},{16,24},{24,16},{1,9},{9,1},{17,25},{25,17},{2,10},{10... | collective-permute-start | bytes 884744 | tf_op jit(solution)/shard_map/ppermute | solution.py:466
  37.1 9.9 %collective-permute-start.9 = (bf16[2,192,384]{2,1,0:T(8,128)(2,1)S(1)}, bf16[2,192,384]{2,1,0:T(8,128)(2,1)S(1)}, u32[]{:S(2)}, u32[]{:S(2)}) collective-permute-start(bf16[2,192,384]{2,1,0:T(8,128)(2,1)S(1)} %pad_maximum_fusion.2.refs_0_), channel_id=1, source_target_pairs={{0,1},{1,0},{2,3},{3,2},{4,5},{5,4},{6,7},{7,6},{8,9},{9,8},{10,11... | collective-permute-start | bytes 884744 | tf_op jit(solution)/shard_map/ppermute | solution.py:470
  40.1 10.0 %collective-permute-start.1 = (bf16[2,192,384]{2,1,0:T(8,128)(2,1)S(1)}, bf16[2,192,384]{2,1,0:T(8,128)(2,1)S(1)}, u32[]{:S(2)}, u32[]{:S(2)}) collective-permute-start(bf16[2,192,384]{2,1,0:T(8,128)(2,1)S(1)} %pad_maximum_fusion.2.refs_0_), channel_id=1, source_target_pairs={{0,8},{8,0},{16,24},{24,16},{1,9},{9,1},{17,25},{25,17},{2,10},{10... | collective-permute-start | bytes 884744 | tf_op jit(solution)/shard_map/ppermute | solution.py:466
  40.2 17.8 %collective-permute-start.26 = (bf16[2,240,384]{2,1,0:T(8,128)(2,1)S(1)}, bf16[2,240,384]{2,1,0:T(8,128)(2,1)S(1)}, u32[]{:S(2)}, u32[]{:S(2)}) collective-permute-start(bf16[2,240,384]{2,1,0:T(8,128)(2,1)S(1)} %pad_maximum_fusion.refs_0_), channel_id=1, source_target_pairs={{0,1},{1,0},{2,3},{3,2},{4,5},{5,4},{6,7},{7,6},{8,9},{9,8},{10,11... | collective-permute-start | bytes 1105928 | tf_op jit(solution)/shard_map/ppermute | solution.py:470
  40.8 10.9 %collective-permute-start.37 = (bf16[96,768]{1,0:T(8,128)(2,1)S(1)}, bf16[96,768]{1,0:T(8,128)(2,1)S(1)}, u32[]{:S(2)}, u32[]{:S(2)}) collective-permute-start(bf16[96,768]{1,0:T(8,128)(2,1)S(1)} %bitcast.152), channel_id=1, source_target_pairs={{0,6},{1,7},{2,4},{3,5},{4,2},{5,3},{6,0},{7,1},{8,14},{9,15},{10,... | collective-permute-start | bytes 442376 | tf_op jit(solution)/shard_map/ppermute | solution.py:470
  47.3 9.7 %collective-permute-start.34 = (bf16[96,768]{1,0:T(8,128)(2,1)S(1)}, bf16[96,768]{1,0:T(8,128)(2,1)S(1)}, u32[]{:S(2)}, u32[]{:S(2)}) collective-permute-start(bf16[96,768]{1,0:T(8,128)(2,1)S(1)} %bitcast.154), channel_id=1, source_target_pairs={{0,2},{1,3},{2,0},{3,1},{4,6},{5,7},{6,4},{7,5},{8,10},{9,11},{10,... | collective-permute-start | bytes 442376 | tf_op jit(solution)/shard_map/ppermute | solution.py:470
  55.5 9.9 %collective-permute-start.28 = (bf16[2,240,384]{2,1,0:T(8,128)(2,1)S(1)}, bf16[2,240,384]{2,1,0:T(8,128)(2,1)S(1)}, u32[]{:S(2)}, u32[]{:S(2)}) collective-permute-start(bf16[2,240,384]{2,1,0:T(8,128)(2,1)S(1)} %pad_maximum_fusion.1.refs_2_), channel_id=1, source_target_pairs={{0,1},{1,0},{2,3},{3,2},{4,5},{5,4},{6,7},{7,6},{8,9},{9,8},{10,11... | collective-permute-start | bytes 1105928 | tf_op jit(solution)/shard_map/ppermute | solution.py:470
  57.0 11.6 %collective-permute-start.24 = (bf16[2,240,384]{2,1,0:T(8,128)(2,1)S(1)}, bf16[2,240,384]{2,1,0:T(8,128)(2,1)S(1)}, u32[]{:S(2)}, u32[]{:S(2)}) collective-permute-start(bf16[2,240,384]{2,1,0:T(8,128)(2,1)S(1)} %pad_maximum_fusion.1.refs_2_), channel_id=1, source_target_pairs={{0,16},{8,24},{16,0},{24,8},{1,17},{9,25},{17,1},{25,9},{2,18},{10... | collective-permute-start | bytes 1105928 | tf_op jit(solution)/shard_map/ppermute | solution.py:466
  58.0 10.6 %collective-permute-start.21 = (bf16[2,240,384]{2,1,0:T(8,128)(2,1)S(1)}, bf16[2,240,384]{2,1,0:T(8,128)(2,1)S(1)}, u32[]{:S(2)}, u32[]{:S(2)}) collective-permute-start(bf16[2,240,384]{2,1,0:T(8,128)(2,1)S(1)} %pad_maximum_fusion.1.refs_2_), channel_id=1, source_target_pairs={{0,8},{8,0},{16,24},{24,16},{1,9},{9,1},{17,25},{25,17},{2,10},{10... | collective-permute-start | bytes 1105928 | tf_op jit(solution)/shard_map/ppermute | solution.py:466
  58.3 14.7 %collective-permute-start.15 = (bf16[2,192,384]{2,1,0:T(8,128)(2,1)S(1)}, bf16[2,192,384]{2,1,0:T(8,128)(2,1)S(1)}, u32[]{:S(2)}, u32[]{:S(2)}) collective-permute-start(bf16[2,192,384]{2,1,0:T(8,128)(2,1)S(1)} %collective-permute-done.11.refs_10_), channel_id=1, source_target_pairs={{0,16},{8,24},{16,0},{24,8},{1,17},{9,25},{17,1},{25,9},{2,18},{10... | collective-permute-start | bytes 884744 | tf_op jit(solution)/shard_map/ppermute | solution.py:466
  60.4 12.6 %collective-permute-start.12 = (bf16[2,192,384]{2,1,0:T(8,128)(2,1)S(1)}, bf16[2,192,384]{2,1,0:T(8,128)(2,1)}, u32[]{:S(2)}, u32[]{:S(2)}) collective-permute-start(bf16[2,192,384]{2,1,0:T(8,128)(2,1)S(1)} %collective-permute-done.11.refs_10_), channel_id=1, source_target_pairs={{0,8},{8,0},{16,24},{24,16},{1,9},{9,1},{17,25},{25,17},{2,10},{10... | collective-permute-start | bytes 884744 | tf_op jit(solution)/shard_map/ppermute | solution.py:466
  68.6 9.9 %collective-permute-start.13 = (bf16[2,192,384]{2,1,0:T(8,128)(2,1)S(1)}, bf16[2,192,384]{2,1,0:T(8,128)(2,1)S(1)}, u32[]{:S(2)}, u32[]{:S(2)}) collective-permute-start(bf16[2,192,384]{2,1,0:T(8,128)(2,1)S(1)} %collective-permute-done.5.refs_4_), channel_id=1, source_target_pairs={{0,1},{1,0},{2,3},{3,2},{4,5},{5,4},{6,7},{7,6},{8,9},{9,8},{10,11... | collective-permute-start | bytes 884744 | tf_op jit(solution)/shard_map/ppermute | solution.py:470
  73.0 11.8 %collective-permute-start.43 = (bf16[2,96,768]{2,1,0:T(8,128)(2,1)S(1)}, bf16[2,96,768]{2,1,0:T(8,128)(2,1)S(1)}, u32[]{:S(2)}, u32[]{:S(2)}) collective-permute-start(bf16[2,96,768]{2,1,0:T(8,128)(2,1)S(1)} %pad_maximum_fusion.4.refs_0_), channel_id=1, source_target_pairs={{0,1},{1,0},{2,3},{3,2},{4,5},{5,4},{6,7},{7,6},{8,9},{9,8},{10,11... | collective-permute-start | bytes 884744 | tf_op jit(solution)/shard_map/ppermute | solution.py:470
  74.1 10.7 %collective-permute-start.39 = (bf16[2,96,768]{2,1,0:T(8,128)(2,1)S(1)}, bf16[2,96,768]{2,1,0:T(8,128)(2,1)S(1)}, u32[]{:S(2)}, u32[]{:S(2)}) collective-permute-start(bf16[2,96,768]{2,1,0:T(8,128)(2,1)S(1)} %pad_maximum_fusion.4.refs_0_), channel_id=1, source_target_pairs={{0,16},{8,24},{16,0},{24,8},{1,17},{9,25},{17,1},{25,9},{2,18},{10... | collective-permute-start | bytes 884744 | tf_op jit(solution)/shard_map/ppermute | solution.py:466
  75.7 9.7 %collective-permute-start.35 = (bf16[2,96,768]{2,1,0:T(8,128)(2,1)S(1)}, bf16[2,96,768]{2,1,0:T(8,128)(2,1)S(1)}, u32[]{:S(2)}, u32[]{:S(2)}) collective-permute-start(bf16[2,96,768]{2,1,0:T(8,128)(2,1)S(1)} %pad_maximum_fusion.4.refs_0_), channel_id=1, source_target_pairs={{0,8},{8,0},{16,24},{24,16},{1,9},{9,1},{17,25},{25,17},{2,10},{10... | collective-permute-start | bytes 884744 | tf_op jit(solution)/shard_map/ppermute | solution.py:466
  78.5 12.2 %collective-permute-start.45 = (bf16[2,96,768]{2,1,0:T(8,128)(2,1)S(1)}, bf16[2,96,768]{2,1,0:T(8,128)(2,1)S(1)}, u32[]{:S(2)}, u32[]{:S(2)}) collective-permute-start(bf16[2,96,768]{2,1,0:T(8,128)(2,1)S(1)} %pad_maximum_fusion.5.refs_2_), channel_id=1, source_target_pairs={{0,1},{1,0},{2,3},{3,2},{4,5},{5,4},{6,7},{7,6},{8,9},{9,8},{10,11... | collective-permute-start | bytes 884744 | tf_op jit(solution)/shard_map/ppermute | solution.py:470
  79.0 11.7 %collective-permute-start.41 = (bf16[2,96,768]{2,1,0:T(8,128)(2,1)S(1)}, bf16[2,96,768]{2,1,0:T(8,128)(2,1)S(1)}, u32[]{:S(2)}, u32[]{:S(2)}) collective-permute-start(bf16[2,96,768]{2,1,0:T(8,128)(2,1)S(1)} %pad_maximum_fusion.5.refs_2_), channel_id=1, source_target_pairs={{0,16},{8,24},{16,0},{24,8},{1,17},{9,25},{17,1},{25,9},{2,18},{10... | collective-permute-start | bytes 884744 | tf_op jit(solution)/shard_map/ppermute | solution.py:466
  90.7 9.5 %collective-permute-start.47 = (bf16[2,96,768]{2,1,0:T(8,128)(2,1)S(1)}, bf16[2,96,768]{2,1,0:T(8,128)(2,1)}, u32[]{:S(2)}, u32[]{:S(2)}) collective-permute-start(bf16[2,96,768]{2,1,0:T(8,128)(2,1)S(1)} %collective-permute-done.39.refs_4_), channel_id=1, source_target_pairs={{0,1},{1,0},{2,3},{3,2},{4,5},{5,4},{6,7},{7,6},{8,9},{9,8},{10,11... | collective-permute-start | bytes 884744 | tf_op jit(solution)/shard_map/ppermute | solution.py:470
  91.3 9.0 %collective-permute-start.40 = (bf16[2,96,768]{2,1,0:T(8,128)(2,1)S(1)}, bf16[2,96,768]{2,1,0:T(8,128)(2,1)S(1)}, u32[]{:S(2)}, u32[]{:S(2)}) collective-permute-start(bf16[2,96,768]{2,1,0:T(8,128)(2,1)S(1)} %collective-permute-done.39.refs_4_), channel_id=1, source_target_pairs={{0,8},{8,0},{16,24},{24,16},{1,9},{9,1},{17,25},{25,17},{2,10},{10... | collective-permute-start | bytes 884744 | tf_op jit(solution)/shard_map/ppermute | solution.py:466
  91.4 9.4 %collective-permute-start.49 = (bf16[2,96,768]{2,1,0:T(8,128)(2,1)S(1)}, bf16[2,96,768]{2,1,0:T(8,128)(2,1)}, u32[]{:S(2)}, u32[]{:S(2)}) collective-permute-start(bf16[2,96,768]{2,1,0:T(8,128)(2,1)S(1)} %collective-permute-done.45.refs_10_), channel_id=1, source_target_pairs={{0,16},{8,24},{16,0},{24,8},{1,17},{9,25},{17,1},{25,9},{2,18},{10... | collective-permute-start | bytes 884744 | tf_op jit(solution)/shard_map/ppermute | solution.py:466
  93.2 9.4 %collective-permute-start.46 = (bf16[2,96,768]{2,1,0:T(8,128)(2,1)S(1)}, bf16[2,96,768]{2,1,0:T(8,128)(2,1)S(1)}, u32[]{:S(2)}, u32[]{:S(2)}) collective-permute-start(bf16[2,96,768]{2,1,0:T(8,128)(2,1)S(1)} %collective-permute-done.45.refs_10_), channel_id=1, source_target_pairs={{0,8},{8,0},{16,24},{24,16},{1,9},{9,1},{17,25},{25,17},{2,10},{10... | collective-permute-start | bytes 884744 | tf_op jit(solution)/shard_map/ppermute | solution.py:466
  93.9 8.8 %collective-permute-start.42 = (bf16[2,96,768]{2,1,0:T(8,128)(2,1)S(1)}, bf16[2,96,768]{2,1,0:T(8,128)(2,1)S(1)}, u32[]{:S(2)}, u32[]{:S(2)}) collective-permute-start(bf16[2,96,768]{2,1,0:T(8,128)(2,1)S(1)} %collective-permute-done.41.refs_6_), channel_id=1, source_target_pairs={{0,8},{8,0},{16,24},{24,16},{1,9},{9,1},{17,25},{25,17},{2,10},{10... | collective-permute-start | bytes 884744 | tf_op jit(solution)/shard_map/ppermute | solution.py:466
  100.2 10.3 %collective-permute-start.27 = (bf16[2,240,384]{2,1,0:T(8,128)(2,1)S(1)}, bf16[2,240,384]{2,1,0:T(8,128)(2,1)}, u32[]{:S(2)}, u32[]{:S(2)}) collective-permute-start(bf16[2,240,384]{2,1,0:T(8,128)(2,1)S(1)} %collective-permute-done.26.refs_8_), channel_id=1, source_target_pairs={{0,8},{8,0},{16,24},{24,16},{1,9},{9,1},{17,25},{25,17},{2,10},{10... | collective-permute-start | bytes 1105928 | tf_op jit(solution)/shard_map/ppermute | solution.py:466
  100.2 11.1 %collective-permute-start.30 = (bf16[2,240,384]{2,1,0:T(8,128)(2,1)S(1)}, bf16[2,240,384]{2,1,0:T(8,128)(2,1)}, u32[]{:S(2)}, u32[]{:S(2)}) collective-permute-start(bf16[2,240,384]{2,1,0:T(8,128)(2,1)S(1)} %collective-permute-done.22.refs_4_), channel_id=1, source_target_pairs={{0,1},{1,0},{2,3},{3,2},{4,5},{5,4},{6,7},{7,6},{8,9},{9,8},{10,11... | collective-permute-start | bytes 1105928 | tf_op jit(solution)/shard_map/ppermute | solution.py:470
  100.8 10.8 %collective-permute-start.32 = (bf16[2,240,384]{2,1,0:T(8,128)(2,1)S(1)}, bf16[2,240,384]{2,1,0:T(8,128)(2,1)}, u32[]{:S(2)}, u32[]{:S(2)}) collective-permute-start(bf16[2,240,384]{2,1,0:T(8,128)(2,1)S(1)} %collective-permute-done.28.refs_10_), channel_id=1, source_target_pairs={{0,16},{8,24},{16,0},{24,8},{1,17},{9,25},{17,1},{25,9},{2,18},{10... | collective-permute-start | bytes 1105928 | tf_op jit(solution)/shard_map/ppermute | solution.py:466
  102.6 9.3 %collective-permute-start.48 = (bf16[2,96,768]{2,1,0:T(8,128)(2,1)}, bf16[2,96,768]{2,1,0:T(8,128)(2,1)}, u32[]{:S(2)}, u32[]{:S(2)}) collective-permute-start(bf16[2,96,768]{2,1,0:T(8,128)(2,1)} %collective-permute-done.47.refs_12_), channel_id=1, source_target_pairs={{0,8},{8,0},{16,24},{24,16},{1,9},{9,1},{17,25},{25,17},{2,10},{10... | collective-permute-start | bytes 884744 | tf_op jit(solution)/shard_map/ppermute | solution.py:466
  102.7 9.4 %collective-permute-start.50 = (bf16[2,96,768]{2,1,0:T(8,128)(2,1)}, bf16[2,96,768]{2,1,0:T(8,128)(2,1)}, u32[]{:S(2)}, u32[]{:S(2)}) collective-permute-start(bf16[2,96,768]{2,1,0:T(8,128)(2,1)} %collective-permute-done.49.refs_14_), channel_id=1, source_target_pairs={{0,8},{8,0},{16,24},{24,16},{1,9},{9,1},{17,25},{25,17},{2,10},{10... | collective-permute-start | bytes 884744 | tf_op jit(solution)/shard_map/ppermute | solution.py:466
  110.5 35.5 %collective-permute-start.23 = (bf16[2,240,384]{2,1,0:T(8,128)(2,1)S(1)}, bf16[2,240,384]{2,1,0:T(8,128)(2,1)S(1)}, u32[]{:S(2)}, u32[]{:S(2)}) collective-permute-start(bf16[2,240,384]{2,1,0:T(8,128)(2,1)S(1)} %collective-permute-done.22.refs_4_), channel_id=1, source_target_pairs={{0,8},{8,0},{16,24},{24,16},{1,9},{9,1},{17,25},{25,17},{2,10},{10... | collective-permute-start | bytes 1105928 | tf_op jit(solution)/shard_map/ppermute | solution.py:466
  111.3 34.7 %collective-permute-start.29 = (bf16[2,240,384]{2,1,0:T(8,128)(2,1)S(1)}, bf16[2,240,384]{2,1,0:T(8,128)(2,1)S(1)}, u32[]{:S(2)}, u32[]{:S(2)}) collective-permute-start(bf16[2,240,384]{2,1,0:T(8,128)(2,1)S(1)} %collective-permute-done.28.refs_10_), channel_id=1, source_target_pairs={{0,8},{8,0},{16,24},{24,16},{1,9},{9,1},{17,25},{25,17},{2,10},{10... | collective-permute-start | bytes 1105928 | tf_op jit(solution)/shard_map/ppermute | solution.py:466
  111.6 34.4 %collective-permute-start.25 = (bf16[2,240,384]{2,1,0:T(8,128)(2,1)S(1)}, bf16[2,240,384]{2,1,0:T(8,128)(2,1)S(1)}, u32[]{:S(2)}, u32[]{:S(2)}) collective-permute-start(bf16[2,240,384]{2,1,0:T(8,128)(2,1)S(1)} %copy-done.14), channel_id=1, source_target_pairs={{0,8},{8,0},{16,24},{24,16},{1,9},{9,1},{17,25},{25,17},{2,10},{10... | collective-permute-start | bytes 1105928 | tf_op jit(solution)/shard_map/ppermute | solution.py:466
  111.9 34.2 %collective-permute-start.31 = (bf16[2,240,384]{2,1,0:T(8,128)(2,1)}, bf16[2,240,384]{2,1,0:T(8,128)(2,1)S(1)}, u32[]{:S(2)}, u32[]{:S(2)}) collective-permute-start(bf16[2,240,384]{2,1,0:T(8,128)(2,1)} %collective-permute-done.30.refs_12_), channel_id=1, source_target_pairs={{0,8},{8,0},{16,24},{24,16},{1,9},{9,1},{17,25},{25,17},{2,10},{10... | collective-permute-start | bytes 1105928 | tf_op jit(solution)/shard_map/ppermute | solution.py:466
  112.2 33.9 %collective-permute-start.33 = (bf16[2,240,384]{2,1,0:T(8,128)(2,1)}, bf16[2,240,384]{2,1,0:T(8,128)(2,1)S(1)}, u32[]{:S(2)}, u32[]{:S(2)}) collective-permute-start(bf16[2,240,384]{2,1,0:T(8,128)(2,1)} %collective-permute-done.32.refs_14_), channel_id=1, source_target_pairs={{0,8},{8,0},{16,24},{24,16},{1,9},{9,1},{17,25},{25,17},{2,10},{10... | collective-permute-start | bytes 1105928 | tf_op jit(solution)/shard_map/ppermute | solution.py:466
  266.6 38.4 %collective-permute-start.51 = (bf16[2,2,4,192,384]{4,3,2,1,0:T(8,128)(2,1)}, bf16[2,2,4,192,384]{4,3,2,1,0:T(8,128)(2,1)}, u32[]{:S(2)}, u32[]{:S(2)}) collective-permute-start(bf16[2,2,4,192,384]{4,3,2,1,0:T(8,128)(2,1)} %get-tuple-element.67), channel_id=1, source_target_pairs={{0,8},{8,0},{16,24},{24,16},{1,9},{9,1},{17,25},{25,17},{2,10},{10... | collective-permute-start | bytes 7077896 | tf_op jit(solution)/shard_map/ppermute | solution.py:466
  278.0 31.3 %collective-permute-start.67 = (bf16[2,2,4,96,768]{4,3,2,1,0:T(8,128)(2,1)}, bf16[2,2,4,96,768]{4,3,2,1,0:T(8,128)(2,1)S(1)}, u32[]{:S(2)}, u32[]{:S(2)}) collective-permute-start(bf16[2,2,4,96,768]{4,3,2,1,0:T(8,128)(2,1)} %get-tuple-element.74), channel_id=1, source_target_pairs={{0,8},{8,0},{16,24},{24,16},{1,9},{9,1},{17,25},{25,17},{2,10},{10... | collective-permute-start | bytes 7077896 | tf_op jit(solution)/shard_map/ppermute | solution.py:466
  294.4 44.7 %collective-permute-start.59 = (bf16[2,2,4,240,384]{4,3,2,1,0:T(8,128)(2,1)}, bf16[2,2,4,240,384]{4,3,2,1,0:T(8,128)(2,1)S(1)}, u32[]{:S(2)}, u32[]{:S(2)}) collective-permute-start(bf16[2,2,4,240,384]{4,3,2,1,0:T(8,128)(2,1)} %get-tuple-element.72), channel_id=1, source_target_pairs={{0,8},{8,0},{16,24},{24,16},{1,9},{9,1},{17,25},{25,17},{2,10},{10... | collective-permute-start | bytes 8847368 | tf_op jit(solution)/shard_map/ppermute | solution.py:466
  307.5 16.2 %collective-permute-start.52 = (bf16[2,2,192,384]{3,2,1,0:T(8,128)(2,1)S(1)}, bf16[2,2,192,384]{3,2,1,0:T(8,128)(2,1)S(1)}, u32[]{:S(2)}, u32[]{:S(2)}) collective-permute-start(bf16[2,2,192,384]{3,2,1,0:T(8,128)(2,1)S(1)} %slice_bitcast_fusion.10), channel_id=1, source_target_pairs={{0,16},{8,24},{16,0},{24,8},{1,17},{9,25},{17,1},{25,9},{2,18},{10... | collective-permute-start | bytes 1769480 | tf_op jit(solution)/shard_map/ppermute | solution.py:466
  309.2 16.3 %collective-permute-start.55 = (bf16[2,2,192,384]{3,2,1,0:T(8,128)(2,1)S(1)}, bf16[2,2,192,384]{3,2,1,0:T(8,128)(2,1)S(1)}, u32[]{:S(2)}, u32[]{:S(2)}) collective-permute-start(bf16[2,2,192,384]{3,2,1,0:T(8,128)(2,1)S(1)} %slice_bitcast_fusion.8), channel_id=1, source_target_pairs={{0,1},{1,0},{2,3},{3,2},{4,5},{5,4},{6,7},{7,6},{8,9},{9,8},{10,11... | collective-permute-start | bytes 1769480 | tf_op jit(solution)/shard_map/ppermute | solution.py:470
  310.0 26.3 %collective-permute-start.68 = (bf16[2,2,96,768]{3,2,1,0:T(8,128)(2,1)S(1)}, bf16[2,2,96,768]{3,2,1,0:T(8,128)(2,1)S(1)}, u32[]{:S(2)}, u32[]{:S(2)}) collective-permute-start(bf16[2,2,96,768]{3,2,1,0:T(8,128)(2,1)S(1)} %slice_bitcast_fusion.6), channel_id=1, source_target_pairs={{0,16},{8,24},{16,0},{24,8},{1,17},{9,25},{17,1},{25,9},{2,18},{10... | collective-permute-start | bytes 1769480 | tf_op jit(solution)/shard_map/ppermute | solution.py:466
  311.5 26.6 %collective-permute-start.71 = (bf16[2,2,96,768]{3,2,1,0:T(8,128)(2,1)S(1)}, bf16[2,2,96,768]{3,2,1,0:T(8,128)(2,1)S(1)}, u32[]{:S(2)}, u32[]{:S(2)}) collective-permute-start(bf16[2,2,96,768]{3,2,1,0:T(8,128)(2,1)S(1)} %slice_bitcast_fusion.4), channel_id=1, source_target_pairs={{0,1},{1,0},{2,3},{3,2},{4,5},{5,4},{6,7},{7,6},{8,9},{9,8},{10,11... | collective-permute-start | bytes 1769480 | tf_op jit(solution)/shard_map/ppermute | solution.py:470
  325.8 16.8 %collective-permute-start.56 = (bf16[2,192,384]{2,1,0:T(8,128)(2,1)S(1)}, bf16[2,192,384]{2,1,0:T(8,128)(2,1)S(1)}, u32[]{:S(2)}, u32[]{:S(2)}) collective-permute-start(bf16[2,192,384]{2,1,0:T(8,128)(2,1)S(1)} %slice_bitcast_fusion.20), channel_id=1, source_target_pairs={{0,16},{8,24},{16,0},{24,8},{1,17},{9,25},{17,1},{25,9},{2,18},{10... | collective-permute-start | bytes 884744 | tf_op jit(solution)/shard_map/ppermute | solution.py:466
  326.3 18.1 %collective-permute-start.53 = (bf16[2,192,384]{2,1,0:T(8,128)(2,1)S(1)}, bf16[2,192,384]{2,1,0:T(8,128)(2,1)S(1)}, u32[]{:S(2)}, u32[]{:S(2)}) collective-permute-start(bf16[2,192,384]{2,1,0:T(8,128)(2,1)S(1)} %slice_bitcast_fusion.22), channel_id=1, source_target_pairs={{0,1},{1,0},{2,3},{3,2},{4,5},{5,4},{6,7},{7,6},{8,9},{9,8},{10,11... | collective-permute-start | bytes 884744 | tf_op jit(solution)/shard_map/ppermute | solution.py:470
  338.5 13.0 %collective-permute-start.72 = (bf16[2,96,768]{2,1,0:T(8,128)(2,1)S(1)}, bf16[2,96,768]{2,1,0:T(8,128)(2,1)S(1)}, u32[]{:S(2)}, u32[]{:S(2)}) collective-permute-start(bf16[2,96,768]{2,1,0:T(8,128)(2,1)S(1)} %slice_bitcast_fusion.16), channel_id=1, source_target_pairs={{0,16},{8,24},{16,0},{24,8},{1,17},{9,25},{17,1},{25,9},{2,18},{10... | collective-permute-start | bytes 884744 | tf_op jit(solution)/shard_map/ppermute | solution.py:466
  338.9 11.8 %collective-permute-start.69 = (bf16[2,96,768]{2,1,0:T(8,128)(2,1)S(1)}, bf16[2,96,768]{2,1,0:T(8,128)(2,1)S(1)}, u32[]{:S(2)}, u32[]{:S(2)}) collective-permute-start(bf16[2,96,768]{2,1,0:T(8,128)(2,1)S(1)} %slice_bitcast_fusion.18), channel_id=1, source_target_pairs={{0,1},{1,0},{2,3},{3,2},{4,5},{5,4},{6,7},{7,6},{8,9},{9,8},{10,11... | collective-permute-start | bytes 884744 | tf_op jit(solution)/shard_map/ppermute | solution.py:470
  339.9 24.2 %collective-permute-start.60 = (bf16[2,2,240,384]{3,2,1,0:T(8,128)(2,1)S(1)}, bf16[2,2,240,384]{3,2,1,0:T(8,128)(2,1)S(1)}, u32[]{:S(2)}, u32[]{:S(2)}) collective-permute-start(bf16[2,2,240,384]{3,2,1,0:T(8,128)(2,1)S(1)} %slice_bitcast_fusion.2), channel_id=1, source_target_pairs={{0,16},{8,24},{16,0},{24,8},{1,17},{9,25},{17,1},{25,9},{2,18},{10... | collective-permute-start | bytes 2211848 | tf_op jit(solution)/shard_map/ppermute | solution.py:466
  342.6 22.8 %collective-permute-start.63 = (bf16[2,2,240,384]{3,2,1,0:T(8,128)(2,1)S(1)}, bf16[2,2,240,384]{3,2,1,0:T(8,128)(2,1)S(1)}, u32[]{:S(2)}, u32[]{:S(2)}) collective-permute-start(bf16[2,2,240,384]{3,2,1,0:T(8,128)(2,1)S(1)} %slice_bitcast_fusion), channel_id=1, source_target_pairs={{0,1},{1,0},{2,3},{3,2},{4,5},{5,4},{6,7},{7,6},{8,9},{9,8},{10,11... | collective-permute-start | bytes 2211848 | tf_op jit(solution)/shard_map/ppermute | solution.py:470
  344.4 23.1 %collective-permute-start.57 = (bf16[192,384]{1,0:T(8,128)(2,1)S(1)}, bf16[192,384]{1,0:T(8,128)(2,1)S(1)}, u32[]{:S(2)}, u32[]{:S(2)}) collective-permute-start(bf16[192,384]{1,0:T(8,128)(2,1)S(1)} %get-tuple-element.89), channel_id=1, source_target_pairs={{0,4},{1,5},{2,6},{3,7},{4,0},{5,1},{6,2},{7,3},{8,12},{9,13},{10,... | collective-permute-start | bytes 442376 | tf_op jit(solution)/shard_map/ppermute | solution.py:470
  350.7 17.3 %collective-permute-start.58 = (bf16[192,384]{1,0:T(8,128)(2,1)S(1)}, bf16[192,384]{1,0:T(8,128)(2,1)S(1)}, u32[]{:S(2)}, u32[]{:S(2)}) collective-permute-start(bf16[192,384]{1,0:T(8,128)(2,1)S(1)} %get-tuple-element.90), channel_id=1, source_target_pairs={{0,6},{1,7},{2,4},{3,5},{4,2},{5,3},{6,0},{7,1},{8,14},{9,15},{10,... | collective-permute-start | bytes 442376 | tf_op jit(solution)/shard_map/ppermute | solution.py:470
  351.5 18.1 %collective-permute-start.54 = (bf16[192,384]{1,0:T(8,128)(2,1)S(1)}, bf16[192,384]{1,0:T(8,128)(2,1)S(1)}, u32[]{:S(2)}, u32[]{:S(2)}) collective-permute-start(bf16[192,384]{1,0:T(8,128)(2,1)S(1)} %slice_bitcast_fusion.34), channel_id=1, source_target_pairs={{0,2},{1,3},{2,0},{3,1},{4,6},{5,7},{6,4},{7,5},{8,10},{9,11},{10,... | collective-permute-start | bytes 442376 | tf_op jit(solution)/shard_map/ppermute | solution.py:470
  364.1 18.3 %collective-permute-start.73 = (bf16[96,768]{1,0:T(8,128)(2,1)S(1)}, bf16[96,768]{1,0:T(8,128)(2,1)S(1)}, u32[]{:S(2)}, u32[]{:S(2)}) collective-permute-start(bf16[96,768]{1,0:T(8,128)(2,1)S(1)} %get-tuple-element.87), channel_id=1, source_target_pairs={{0,4},{1,5},{2,6},{3,7},{4,0},{5,1},{6,2},{7,3},{8,12},{9,13},{10,... | collective-permute-start | bytes 442376 | tf_op jit(solution)/shard_map/ppermute | solution.py:470
  365.4 17.8 %collective-permute-start.74 = (bf16[96,768]{1,0:T(8,128)(2,1)S(1)}, bf16[96,768]{1,0:T(8,128)(2,1)S(1)}, u32[]{:S(2)}, u32[]{:S(2)}) collective-permute-start(bf16[96,768]{1,0:T(8,128)(2,1)S(1)} %get-tuple-element.88), channel_id=1, source_target_pairs={{0,6},{1,7},{2,4},{3,5},{4,2},{5,3},{6,0},{7,1},{8,14},{9,15},{10,... | collective-permute-start | bytes 442376 | tf_op jit(solution)/shard_map/ppermute | solution.py:470
  367.5 15.8 %collective-permute-start.70 = (bf16[96,768]{1,0:T(8,128)(2,1)S(1)}, bf16[96,768]{1,0:T(8,128)(2,1)S(1)}, u32[]{:S(2)}, u32[]{:S(2)}) collective-permute-start(bf16[96,768]{1,0:T(8,128)(2,1)S(1)} %slice_bitcast_fusion.30), channel_id=1, source_target_pairs={{0,2},{1,3},{2,0},{3,1},{4,6},{5,7},{6,4},{7,5},{8,10},{9,11},{10,... | collective-permute-start | bytes 442376 | tf_op jit(solution)/shard_map/ppermute | solution.py:470
  368.1 9.1 %collective-permute-start.64 = (bf16[2,240,384]{2,1,0:T(8,128)(2,1)S(1)}, bf16[2,240,384]{2,1,0:T(8,128)(2,1)S(1)}, u32[]{:S(2)}, u32[]{:S(2)}) collective-permute-start(bf16[2,240,384]{2,1,0:T(8,128)(2,1)S(1)} %slice_bitcast_fusion.12), channel_id=1, source_target_pairs={{0,16},{8,24},{16,0},{24,8},{1,17},{9,25},{17,1},{25,9},{2,18},{10... | collective-permute-start | bytes 1105928 | tf_op jit(solution)/shard_map/ppermute | solution.py:466
  371.6 8.9 %collective-permute-start.61 = (bf16[2,240,384]{2,1,0:T(8,128)(2,1)S(1)}, bf16[2,240,384]{2,1,0:T(8,128)(2,1)S(1)}, u32[]{:S(2)}, u32[]{:S(2)}) collective-permute-start(bf16[2,240,384]{2,1,0:T(8,128)(2,1)S(1)} %slice_bitcast_fusion.14), channel_id=1, source_target_pairs={{0,1},{1,0},{2,3},{3,2},{4,5},{5,4},{6,7},{7,6},{8,9},{9,8},{10,11... | collective-permute-start | bytes 1105928 | tf_op jit(solution)/shard_map/ppermute | solution.py:470
  377.3 14.5 %collective-permute-start.65 = (bf16[240,384]{1,0:T(8,128)(2,1)S(1)}, bf16[240,384]{1,0:T(8,128)(2,1)S(1)}, u32[]{:S(2)}, u32[]{:S(2)}) collective-permute-start(bf16[240,384]{1,0:T(8,128)(2,1)S(1)} %get-tuple-element.85), channel_id=1, source_target_pairs={{0,4},{1,5},{2,6},{3,7},{4,0},{5,1},{6,2},{7,3},{8,12},{9,13},{10,... | collective-permute-start | bytes 552968 | tf_op jit(solution)/shard_map/ppermute | solution.py:470
  380.5 11.3 %collective-permute-start.66 = (bf16[240,384]{1,0:T(8,128)(2,1)S(1)}, bf16[240,384]{1,0:T(8,128)(2,1)S(1)}, u32[]{:S(2)}, u32[]{:S(2)}) collective-permute-start(bf16[240,384]{1,0:T(8,128)(2,1)S(1)} %get-tuple-element.86), channel_id=1, source_target_pairs={{0,6},{1,7},{2,4},{3,5},{4,2},{5,3},{6,0},{7,1},{8,14},{9,15},{10,... | collective-permute-start | bytes 552968 | tf_op jit(solution)/shard_map/ppermute | solution.py:470
  382.4 11.1 %collective-permute-start.62 = (bf16[240,384]{1,0:T(8,128)(2,1)S(1)}, bf16[240,384]{1,0:T(8,128)(2,1)S(1)}, u32[]{:S(2)}, u32[]{:S(2)}) collective-permute-start(bf16[240,384]{1,0:T(8,128)(2,1)S(1)} %slice_bitcast_fusion.26), channel_id=1, source_target_pairs={{0,2},{1,3},{2,0},{3,1},{4,6},{5,7},{6,4},{7,5},{8,10},{9,11},{10,... | collective-permute-start | bytes 552968 | tf_op jit(solution)/shard_map/ppermute | solution.py:470
  (57 other events, 1220.7 us)
